TPU v7x, 32 devices: a whole 2x2x4 slice. The times are simulated.
32 devices in a mesh: group: 2 (over y), row: 8 (over z, x), col: 2 (over core).
Axes of the slice: x: 2, y: 2, z: 4, core: 2. Of those that a mesh axis runs over, the one named last changes fastest.
Arguments:
- pair: bfloat16 [768, 384, 128], P(('group', 'row'), 'col'), parts along dimension 0, may hold values from -16 to 16
- chain_ids: int32 [768], P('group'), parts along dimension 0, may hold values from 0 to 3, never falling along the last dimension, each value on 1 to 192 neighbouring positions
- token_mask: int32 [768], P('group'), parts along dimension 0, may hold values 0 or 1
- same_chain_bias: bfloat16 [128], replicated, may hold values from -4 to 4
- proj_weight: bfloat16 [2, 128, 512], replicated, may hold values from -0.5 to 0.5
- gate_weight: bfloat16 [2, 128, 128], replicated, may hold values from -0.5 to 0.5
- out_weight: bfloat16 [2, 128, 128], replicated, may hold values from -0.5 to 0.5
Outputs:
- updated: bfloat16 [768, 384, 128], P(('group', 'row'), 'col'), parts along dimension 0
There are 2 independent parts, one for each index of `group`. A program takes and returns all parts, laid end to end along the dimension named above; an argument that names none is the same for every part. Nothing has to cross between parts.
Inputs may be any that keep to these rules, and one draw needn't show every extreme that they name: `chain_ids`: chain ids never fall along the residues.
All inputs are finite; a program needn't handle non-finite values.
Results may differ from a plain program's by a relative error of at most 0.0095.
Values may be sent and summed in bfloat16 or wider, within the bound.
A program may use at most 64 MiB of HBM per device.

v0:
```python
import jax
import jax.numpy as jnp
from jax import lax
from jax.sharding import PartitionSpec as P


def layer_norm(values):
    mean = jnp.mean(values, axis=-1, keepdims=True)
    centred = values - mean
    var = jnp.mean(centred * centred, axis=-1, keepdims=True)
    return centred * lax.rsqrt(var + 1e-05)


def make_contract(rows_grid, cols_grid, rows_tile, cols_tile, incoming):

    def contract(pieces):
        items = pieces.shape[2]
        total = rows_grid * rows_tile
        whole = pieces.reshape(rows_grid, cols_grid, 2, items, rows_tile, cols_tile)
        whole = whole.transpose(2, 3, 0, 4, 1, 5).reshape(2, items, total, cols_grid * cols_tile)
        if incoming:
            tri = jnp.einsum("mki,mkj->mij", whole[0], whole[1], preferred_element_type=jnp.float32)
        else:
            tri = jnp.einsum("mik,mjk->mij", whole[0], whole[1], preferred_element_type=jnp.float32)
        tri = tri.astype(jnp.bfloat16)
        tri = tri.reshape(items, rows_grid, rows_tile, cols_grid, cols_tile).transpose(
            1, 3, 0, 2, 4
        )
        return tri.reshape(rows_grid * cols_grid, items, rows_tile * cols_tile)

    return contract


def triangle(pair_now, mask_flat, proj, gate, outw, incoming):
    rows_tile, cols_tile, channels = pair_now.shape
    hidden = proj.shape[1] // 4
    rows_grid = lax.axis_size("row")
    cols_grid = lax.axis_size("col")
    owners = rows_grid * cols_grid
    per_owner = hidden // owners
    cells = rows_tile * cols_tile
    normed = layer_norm(pair_now.astype(jnp.float32)).astype(jnp.bfloat16).reshape(cells, channels)
    proj_out = jnp.dot(normed, proj, preferred_element_type=jnp.float32)
    left = (
        mask_flat * jax.nn.sigmoid(proj_out[:, hidden : 2 * hidden]) * proj_out[:, 0:hidden]
    ).astype(jnp.bfloat16)
    right = (
        mask_flat
        * jax.nn.sigmoid(proj_out[:, 3 * hidden : 4 * hidden])
        * proj_out[:, 2 * hidden : 3 * hidden]
    ).astype(jnp.bfloat16)
    stacked = jnp.stack([left, right]).reshape(2, cells, owners, per_owner).transpose(2, 0, 3, 1)
    contract = make_contract(rows_grid, cols_grid, rows_tile, cols_tile, incoming)
    result = contract(
        lax.all_to_all(stacked, ("row", "col"), split_axis=0, concat_axis=0, tiled=True)
    )
    returned = lax.all_to_all(result, ("row", "col"), split_axis=0, concat_axis=0, tiled=True)
    tri = returned.reshape(hidden, cells).T
    normed_tri = layer_norm(tri.astype(jnp.float32)).astype(jnp.bfloat16)
    update = jnp.dot(normed_tri, outw, preferred_element_type=jnp.float32)
    gating = jax.nn.sigmoid(jnp.dot(normed, gate, preferred_element_type=jnp.float32))
    result_flat = pair_now.reshape(cells, channels).astype(jnp.float32) + gating * update
    return result_flat.astype(jnp.bfloat16).reshape(rows_tile, cols_tile, channels)


def shards(pair, chain_ids, token_mask, same_chain_bias, proj_weight, gate_weight, out_weight):
    rows_tile, cols_tile, channels = pair.shape
    row_index = lax.axis_index("row")
    col_index = lax.axis_index("col")
    row_start = row_index * rows_tile
    col_start = col_index * cols_tile
    chain_rows = lax.dynamic_slice_in_dim(chain_ids, row_start, rows_tile)
    chain_cols = lax.dynamic_slice_in_dim(chain_ids, col_start, cols_tile)
    mask_rows = lax.dynamic_slice_in_dim(token_mask, row_start, rows_tile).astype(jnp.float32)
    mask_cols = lax.dynamic_slice_in_dim(token_mask, col_start, cols_tile).astype(jnp.float32)
    same = (chain_rows[:, None] == chain_cols[None, :]).astype(jnp.float32)
    start = (
        pair.astype(jnp.float32)
        + same[:, :, None] * same_chain_bias.astype(jnp.float32)[None, None, :]
    ).astype(jnp.bfloat16)
    mask_flat = (mask_rows[:, None] * mask_cols[None, :]).reshape(rows_tile * cols_tile, 1)
    first = triangle(start, mask_flat, proj_weight[0], gate_weight[0], out_weight[0], False)
    return triangle(first, mask_flat, proj_weight[1], gate_weight[1], out_weight[1], True)


def solution(mesh):
    return jax.shard_map(
        shards,
        mesh=mesh,
        in_specs=(P(("group", "row"), "col", None), P("group"), P("group"), P(), P(), P(), P()),
        out_specs=P(("group", "row"), "col", None),
        check_vma=False,
    )
```

profile of v0, /device:TPU:15, one launch (start us, length us, event | category | flops | bytes accessed | tf_op | source)
XLA Modules:
  0.0 532.7 jit_solution(9814449672120905748)
XLA Ops:
  0.0 0.9 dynamic_slice.12
  0.9 0.8 dynamic_slice.13
  1.7 0.8 dynamic-slice_convert_fusion.1
  2.4 0.8 dynamic-slice_convert_fusion
  3.2 0.7 convert_element_type.93
  3.8 0.1 compare_convert_fusion
  3.9 4.4 convert_reduce_fusion.2
  8.3 6.2 %multiply_reduce_fusion.1 = f32[48,192]{1,0:T(8,128)S(1)} fusion(f32[48,192]{1,0:T(8,128)S(1)} %broadcast_multiply_fusion.1, f32[128]{0:T(128)S(1)} %convert_element_type.93, f32[48,192]{1,0:T(8,128)S(1)} %compare_convert_fusion, bf16[48,192,128]{2,1,0:T(8,128)(2,1)} %param.7), kind=kLoop, calls=%fused_computation.64 | loop fusion | flops 9427968 | bytes 2470400 | tf_op jit(solution)/shard_map/reduce_sum | solution.py:10
  14.6 0.0 copy-done.1
  14.6 0.0 copy-start.4
  14.6 6.7 %multiply_convert_fusion.1 = (bf16[48,192,128]{2,1,0:T(8,128)(2,1)}, f32[48,192,128]{2,1,0:T(8,128)}) fusion(f32[48,192]{1,0:T(8,128)S(1)} %add_rsqrt_fusion, f32[48,192]{1,0:T(8,128)S(1)} %broadcast_multiply_fusion.1, f32[128]{0:T(128)S(1)} %convert_element_type.93, f32[48,192]{1,0:T(8,128)S(1)} %compare_convert_fusion, bf16[48,192,128]{2,1,0:T(8,128)(2,1)S(1)} %copy-done.1), kind=kLoop, calls=%fused_computation.63 | loop fusion | flops 9437184 | bytes 9548288 | tf_op jit(solution)/shard_map/convert_element_type | solution.py:42
  21.3 0.1 broadcast_multiply_fusion
  21.4 0.1 mul.144
  21.5 0.0 copy-done.4
  21.5 4.3 fusion.50
  25.8 5.1 fusion.36
  30.8 4.4 copy.38
  35.2 2.5 copy.41
  37.7 2.8 maximum_bitcast_fusion
  40.5 0.4 copy.42
  40.9 110.1 %all_to_all.20 = bf16[16,2,8,9216]{3,2,1,0:T(8,128)(2,1)} all-to-all(bf16[16,2,8,9216]{3,2,1,0:T(8,128)(2,1)S(1)} %copy.42), channel_id=1, replica_groups=mesh['group'=2,'row'=8,'col'=2] {'row','col'}, dimensions={0} | all-to-all | bytes 9437184 | tf_op jit(solution)/shard_map/all_to_all | solution.py:55
  151.0 10.7 %reshape.160 = bf16[8,2,2,8,48,192]{5,4,3,2,1,0:T(8,128)(2,1)} reshape(bf16[16,2,8,9216]{3,2,1,0:T(8,128)(2,1)} %all_to_all.20) | data formatting | bytes 9437184 | tf_op jit(solution)/shard_map/reshape | solution.py:19
  161.7 11.9 %copy.63 = bf16[8,2,2,8,48,192]{5,1,4,0,3,2:T(2,128)(2,1)S(1)} copy(bf16[8,2,2,8,48,192]{5,4,3,2,1,0:T(8,128)(2,1)} %reshape.160) | data formatting | bytes 9437184 | tf_op jit(solution)/shard_map/reshape | solution.py:19
  173.7 6.3 %fusion.63 = (bf16[1,8,8,48,2,192]{5,4,3,2,1,0:T(2,128)(2,1)S(1)}, bf16[1,8,8,48,2,192]{5,4,3,2,1,0:T(2,128)(2,1)}) fusion(bf16[2,8,8,48,2,192]{5,4,3,2,1,0:T(2,128)(2,1)S(1)} %bitcast.85), kind=kLoop, calls=%fused_computation.103 | loop fusion | bytes 9437184 | tf_op jit(solution)/shard_map/slice | solution.py:24
  180.0 7.4 %squeeze.32 = bf16[8,384,384]{2,1,0:T(8,128)(2,1)} reshape(bf16[1,8,8,48,2,192]{5,4,3,2,1,0:T(2,128)(2,1)} %get-tuple-element.12) | data formatting | bytes 4718592 | tf_op jit(solution)/shard_map/squeeze | solution.py:24
  187.4 2.9 squeeze.33
  190.3 5.6 %convolution_convert_fusion.1 = bf16[8,384,384]{2,1,0:T(8,128)(2,1)} fusion(bf16[8,384,384]{2,1,0:T(8,128)(2,1)} %squeeze.32, bf16[8,384,384]{2,1,0:T(8,128)(2,1)} %squeeze.33), kind=kOutput, calls=%fused_computation.74 | convolution fusion | flops 907149312 | bytes 7077888 | tf_op jit(solution)/shard_map/mik,mjk->mij/dot_general | solution.py:24
  195.8 7.2 %reshape.161 = bf16[8,8,48,2,192]{4,3,2,1,0:T(2,128)(2,1)S(1)} reshape(bf16[8,384,384]{2,1,0:T(8,128)(2,1)} %convolution_convert_fusion.1) | data formatting | bytes 4718592 | tf_op jit(solution)/shard_map/reshape | solution.py:26
  203.0 2.2 copy.65
  205.2 6.2 %reshape.162 = bf16[16,8,9216]{2,1,0:T(8,128)(2,1)} reshape(bf16[8,2,8,48,192]{4,3,2,1,0:T(8,128)(2,1)} %bitcast.88) | data formatting | bytes 4718592 | tf_op jit(solution)/shard_map/reshape | solution.py:29
  211.4 5.6 %all-to-all-start.1 = ((bf16[16,8,9216]{2,1,0:T(8,128)(2,1)}), bf16[16,8,9216]{2,1,0:T(8,128)(2,1)S(1)}, u32[]{:S(2)}, u32[]{:S(2)}) async-start(bf16[16,8,9216]{2,1,0:T(8,128)(2,1)} %reshape.162), calls=%async_computation.1 | async-start | bytes 4718592 | tf_op jit(solution)/shard_map/all_to_all | solution.py:57
  217.1 0.0 copy-done.7
  217.1 5.2 fusion.9
  222.3 47.7 %all-to-all-done.1 = bf16[16,8,9216]{2,1,0:T(8,128)(2,1)S(1)} async-done(((bf16[16,8,9216]{2,1,0:T(8,128)(2,1)}), bf16[16,8,9216]{2,1,0:T(8,128)(2,1)S(1)}, u32[]{:S(2)}, u32[]{:S(2)}) %all-to-all-start.1) | async-done | bytes 2359328 | tf_op jit(solution)/shard_map/all_to_all | solution.py:57
  270.0 0.4 convert_reduce_fusion.1
  270.4 0.7 fusion.14
  271.1 1.2 copy-done.3
  272.3 4.6 fusion.64
  277.0 0.0 copy-start
  277.0 2.7 multiply_reduce_fusion
  279.8 2.7 fusion.48
  282.4 5.1 fusion.26
  287.5 4.4 copy.47
  291.9 2.4 copy.50
  294.3 2.8 maximum_bitcast_fusion.1
  297.1 0.4 copy.51
  297.5 108.6 %all_to_all.21 = bf16[16,2,8,9216]{3,2,1,0:T(8,128)(2,1)} all-to-all(bf16[16,2,8,9216]{3,2,1,0:T(8,128)(2,1)S(1)} %copy.51), channel_id=1, replica_groups=mesh['group'=2,'row'=8,'col'=2] {'row','col'}, dimensions={0} | all-to-all | bytes 9437184 | tf_op jit(solution)/shard_map/all_to_all | solution.py:55
  406.0 10.7 %reshape.163 = bf16[8,2,2,8,48,192]{5,4,3,2,1,0:T(8,128)(2,1)} reshape(bf16[16,2,8,9216]{3,2,1,0:T(8,128)(2,1)} %all_to_all.21) | data formatting | bytes 9437184 | tf_op jit(solution)/shard_map/reshape | solution.py:19
  416.8 11.9 %copy.62 = bf16[8,2,2,8,48,192]{5,1,4,0,3,2:T(2,128)(2,1)S(1)} copy(bf16[8,2,2,8,48,192]{5,4,3,2,1,0:T(8,128)(2,1)} %reshape.163) | data formatting | bytes 9437184 | tf_op jit(solution)/shard_map/reshape | solution.py:19
  428.7 6.3 %fusion.62 = (bf16[1,8,8,48,2,192]{5,4,3,2,1,0:T(2,128)(2,1)S(1)}, bf16[1,8,8,48,2,192]{5,4,3,2,1,0:T(2,128)(2,1)}) fusion(bf16[2,8,8,48,2,192]{5,4,3,2,1,0:T(2,128)(2,1)S(1)} %bitcast.86), kind=kLoop, calls=%fused_computation.102 | loop fusion | bytes 9437184 | tf_op jit(solution)/shard_map/slice | solution.py:22
  435.0 7.4 %squeeze.37 = bf16[8,384,384]{2,1,0:T(8,128)(2,1)} reshape(bf16[1,8,8,48,2,192]{5,4,3,2,1,0:T(2,128)(2,1)} %get-tuple-element.10) | data formatting | bytes 4718592 | tf_op jit(solution)/shard_map/squeeze | solution.py:22
  442.4 2.9 squeeze.38
  445.3 5.4 %convolution_convert_fusion = bf16[8,384,384]{2,1,0:T(8,128)(2,1)} fusion(bf16[8,384,384]{2,1,0:T(8,128)(2,1)} %squeeze.37, bf16[8,384,384]{2,1,0:T(8,128)(2,1)} %squeeze.38), kind=kOutput, calls=%fused_computation.73 | convolution fusion | flops 907149312 | bytes 7077888 | tf_op jit(solution)/shard_map/mki,mkj->mij/dot_general | solution.py:22
  450.7 7.2 %reshape.164 = bf16[8,8,48,2,192]{4,3,2,1,0:T(2,128)(2,1)S(1)} reshape(bf16[8,384,384]{2,1,0:T(8,128)(2,1)} %convolution_convert_fusion) | data formatting | bytes 4718592 | tf_op jit(solution)/shard_map/reshape | solution.py:26
  457.9 2.2 copy.64
  460.1 6.2 %reshape.165 = bf16[16,8,9216]{2,1,0:T(8,128)(2,1)} reshape(bf16[8,2,8,48,192]{4,3,2,1,0:T(8,128)(2,1)} %bitcast.89) | data formatting | bytes 4718592 | tf_op jit(solution)/shard_map/reshape | solution.py:29
  466.3 5.3 all-to-all-start.3
  471.6 0.0 copy-done.8
  471.6 6.6 %fusion.10 = f32[9216,128]{1,0:T(8,128)} fusion(bf16[2,128,128]{2,1,0:T(8,128)(2,1)S(1)} %copy-done.8, f32[9216,128]{1,0:T(8,128)} %copy-done, f32[9216]{0:T(1024)S(1)} %add_rsqrt_fusion.2, f32[9216]{0:T(1024)S(1)} %broadcast_multiply_fusion.3), kind=kOutput, calls=%fused_computation.14 | convolution fusion | flops 309067776 | bytes 9543680 | tf_op jit(solution)/shard_map/dot_general | solution.py:61
  478.2 46.5 %all-to-all-done.3 = bf16[16,8,9216]{2,1,0:T(8,128)(2,1)S(1)} async-done(((bf16[16,8,9216]{2,1,0:T(8,128)(2,1)}), bf16[16,8,9216]{2,1,0:T(8,128)(2,1)S(1)}, u32[]{:S(2)}, u32[]{:S(2)}) %all-to-all-start.3) | async-done | bytes 2359328 | tf_op jit(solution)/shard_map/all_to_all | solution.py:57
  524.6 0.4 convert_reduce_fusion
  525.0 0.7 fusion.19
  525.8 1.2 copy-done.2
  527.0 5.3 fusion.7
  (18 shorter events, 0.1 us)
Async XLA Ops:
  0.0 14.6 %copy-start.1 = (bf16[48,192,128]{2,1,0:T(8,128)(2,1)S(1)}, bf16[48,192,128]{2,1,0:T(8,128)(2,1)}, u32[]{:S(2)}) copy-start(bf16[48,192,128]{2,1,0:T(8,128)(2,1)} %param.7) | copy-start | bytes 7077892
  14.6 6.9 %copy-start.4 = (bf16[2,128,512]{2,1,0:T(8,128)(2,1)S(1)}, bf16[2,128,512]{2,1,0:T(8,128)(2,1)}, u32[]{:S(2)}) copy-start(bf16[2,128,512]{2,1,0:T(8,128)(2,1)} %param.11) | copy-start | bytes 786436
  205.2 11.8 %copy-start.7 = (bf16[2,128,128]{2,1,0:T(8,128)(2,1)S(1)}, bf16[2,128,128]{2,1,0:T(8,128)(2,1)}, u32[]{:S(2)}) copy-start(bf16[2,128,128]{2,1,0:T(8,128)(2,1)} %param.12) | copy-start | bytes 196612
  211.4 58.6 %all-to-all-start.1 = ((bf16[16,8,9216]{2,1,0:T(8,128)(2,1)}), bf16[16,8,9216]{2,1,0:T(8,128)(2,1)S(1)}, u32[]{:S(2)}, u32[]{:S(2)}) async-start(bf16[16,8,9216]{2,1,0:T(8,128)(2,1)} %reshape.162), calls=%async_computation.1 | async-start | bytes 4718592 | tf_op jit(solution)/shard_map/all_to_all | solution.py:57
  222.3 48.8 %copy-start.5 = (bf16[2,128,128]{2,1,0:T(8,128)(2,1)S(1)}, bf16[2,128,128]{2,1,0:T(8,128)(2,1)}, u32[]{:S(2)}) copy-start(bf16[2,128,128]{2,1,0:T(8,128)(2,1)} %param.13) | copy-start | bytes 196612
  270.0 2.3 copy-start.3
  277.0 5.4 %copy-start = (f32[9216,128]{1,0:T(8,128)}, f32[9216,128]{1,0:T(8,128)S(1)}, u32[]{:S(2)}) copy-start(f32[9216,128]{1,0:T(8,128)S(1)} %get-tuple-element.16) | copy-start | bytes 14155780
  460.1 11.5 %copy-start.8 = (bf16[2,128,128]{2,1,0:T(8,128)(2,1)S(1)}, bf16[2,128,128]{2,1,0:T(8,128)(2,1)}, u32[]{:S(2)}) copy-start(bf16[2,128,128]{2,1,0:T(8,128)(2,1)} %param.12) | copy-start | bytes 196612
  466.3 58.4 %all-to-all-start.3 = ((bf16[16,8,9216]{2,1,0:T(8,128)(2,1)}), bf16[16,8,9216]{2,1,0:T(8,128)(2,1)S(1)}, u32[]{:S(2)}, u32[]{:S(2)}) async-start(bf16[16,8,9216]{2,1,0:T(8,128)(2,1)} %reshape.165), calls=%async_computation.3 | async-start | bytes 4718592 | tf_op jit(solution)/shard_map/all_to_all | solution.py:57
  478.2 47.6 %copy-start.6 = (bf16[2,128,128]{2,1,0:T(8,128)(2,1)S(1)}, bf16[2,128,128]{2,1,0:T(8,128)(2,1)}, u32[]{:S(2)}) copy-start(bf16[2,128,128]{2,1,0:T(8,128)(2,1)} %param.13) | copy-start | bytes 196612
  524.6 2.3 copy-start.2
where the time goes:
time: 540 us; the launch traced here: 533 us
  blocking collectives  219 us (41%)
  local copies, waits for them, and re-layouts  128 us (24%)
  waiting for transfers between devices  94.2 us (17%)
  other arithmetic  40.3 us (7%)
  matrix products  39.5 us (7%)
  starting transfers between devices  10.9 us (2%)
    all_to_all x2, blocking collectives, triangle(): lax.all_to_all(stacked, ('row', 'col'), split_axis=0, concat_axis=0, tile...  219 us
    all_to_all x2, waiting for transfers between devices, triangle(): lax.all_to_all(result, ('row', 'col'), split_axis=0, concat_axis=0, tiled...  94.2 us
    reshape x4, local copies, waits for them, and re-layouts, contract(): whole = pieces.reshape(rows_grid, cols_grid, 2, items, rows_tile, cols_tile)  45.3 us
    reshape x4, local copies, waits for them, and re-layouts, contract(): tri.reshape(items, rows_grid, rows_tile, cols_grid, cols_tile)  18.8 us
    squeeze x2, local copies, waits for them, and re-layouts, contract(): whole[0]  14.8 us
    slice x2, local copies, waits for them, and re-layouts, contract(): whole[1]  12.7 us
    reshape x2, local copies, waits for them, and re-layouts, contract(): return tri.reshape(rows_grid * cols_grid, items, rows_tile * cols_tile)  12.4 us
    dot_general x2, matrix products, triangle(): jnp.dot(normed, gate, preferred_element_type=jnp.float32)  11.8 us
  transfers between devices with their start and end apart: 2, of which 2 were waited for; matrix products, arithmetic and copies ran while one was open for 2% of the time, Pallas kernels for 0%

commit v1 on v0

--- a/solution.py
+++ b/solution.py
@@ -1,7 +1,14 @@
+import functools
+
 import jax
 import jax.numpy as jnp
 from jax import lax
+from jax.experimental import pallas as pl
+from jax.experimental.pallas import tpu as pltpu
 from jax.sharding import PartitionSpec as P
+
+MESH = pl.DeviceIdType.MESH
+CHUNKS = 3
 
 
 def layer_norm(values):
@@ -83,9 +90,381 @@
     return triangle(first, mask_flat, proj_weight[1], gate_weight[1], out_weight[1], True)
 
 
+def sigmoid(values):
+    return 0.5 * jnp.tanh(0.5 * values) + 0.5
+
+
+def normalise(values, axis):
+    mean = jnp.mean(values, axis=axis, keepdims=True)
+    centred = values - mean
+    var = jnp.mean(centred * centred, axis=axis, keepdims=True)
+    return (centred * lax.rsqrt(var + 1e-05)).astype(jnp.bfloat16)
+
+
+def fused_kernel(
+    rows_grid,
+    pair_ref,
+    chain_s,
+    mask_s,
+    chain_v,
+    mask_v,
+    bias_v,
+    proj_v,
+    gate_v,
+    outw_v,
+    out_ref,
+    cells,
+    normed,
+    outbox,
+    inbox,
+    wide,
+    products,
+    back_out,
+    back_in,
+    pair_sems,
+    fwd_send,
+    fwd_recv,
+    back_send,
+    back_recv,
+    own_sems,
+    out_sems,
+):
+    owners = 2 * rows_grid
+    rows, tokens, _ = cells.shape
+    half = tokens // 2
+    per = inbox.shape[1] // 2
+    step_rows = rows // CHUNKS
+    tiles = tokens // 128
+    row, col = lax.axis_index("row"), lax.axis_index("col")
+    me = row * 2 + col
+    sibling = {"row": row, "col": 1 - col}
+    mine = pl.multiple_of(col * half, half)
+    theirs = pl.multiple_of((1 - col) * half, half)
+
+    def place(owner):
+        return {"row": owner // 2, "col": owner % 2}
+
+    barrier = pltpu.get_barrier_semaphore()
+
+    def greet(step, carry):
+        pl.semaphore_signal(
+            barrier, inc=1, device_id=place((me + step) % owners), device_id_type=MESH
+        )
+        return carry
+
+    lax.fori_loop(1, owners, greet, 0)
+    pl.semaphore_wait(barrier, owners - 1)
+
+    keep = pltpu.make_async_copy(
+        pair_ref.at[pl.ds(col * rows, rows)], cells.at[:, pl.ds(mine, half)], pair_sems.at[0]
+    )
+    swap = pltpu.make_async_remote_copy(
+        src_ref=pair_ref.at[pl.ds((1 - col) * rows, rows)],
+        dst_ref=cells.at[:, pl.ds(mine, half)],
+        send_sem=pair_sems.at[1],
+        recv_sem=pair_sems.at[2],
+        device_id=sibling,
+        device_id_type=MESH,
+    )
+    keep.start()
+    swap.start()
+    keep.wait()
+    swap.wait()
+
+    def fwd_copy(chunk, owner, source):
+        return pltpu.make_async_remote_copy(
+            src_ref=outbox.at[owner, pl.ds(chunk * step_rows, step_rows)],
+            dst_ref=inbox.at[pl.ds(source * rows + chunk * step_rows, step_rows)],
+            send_sem=fwd_send.at[chunk, owner],
+            recv_sem=fwd_recv.at[chunk, source],
+            device_id=place(owner),
+            device_id_type=MESH,
+        )
+
+    def fwd_own(chunk):
+        return pltpu.make_async_copy(
+            outbox.at[me, pl.ds(chunk * step_rows, step_rows)],
+            inbox.at[pl.ds(me * rows + chunk * step_rows, step_rows)],
+            own_sems.at[0, chunk],
+        )
+
+    back_rows = step_rows * per
+
+    def back_copy(chunk, target, source):
+        return pltpu.make_async_remote_copy(
+            src_ref=back_out.at[target, pl.ds(chunk * back_rows, back_rows)],
+            dst_ref=back_in.at[source, pl.ds(chunk * back_rows, back_rows)],
+            send_sem=back_send.at[chunk, target],
+            recv_sem=back_recv.at[chunk, source],
+            device_id=place(target),
+            device_id_type=MESH,
+        )
+
+    def back_own(chunk):
+        return pltpu.make_async_copy(
+            back_out.at[me, pl.ds(chunk * back_rows, back_rows)],
+            back_in.at[me, pl.ds(chunk * back_rows, back_rows)],
+            own_sems.at[1, chunk],
+        )
+
+    def produce(update, chunk):
+        def one_row(step, carry):
+            at = chunk * step_rows + step
+            token = row * (2 * rows) + col * rows + at
+            values = cells[at].astype(jnp.float32)
+            if update == 0:
+                same = chain_v[...] == chain_s[token]
+                start = (values + jnp.where(same, bias_v[...], 0.0)).astype(jnp.bfloat16)
+                cells[at] = start
+                values = start.astype(jnp.float32)
+            flat = normalise(values, 1)
+            normed[at] = flat
+            proj = lax.dot_general(
+                proj_v[update],
+                flat,
+                (((1,), (1,)), ((), ())),
+                preferred_element_type=jnp.float32,
+            )
+            width = proj.shape[0] // 2
+            mask = mask_s[token] * mask_v[...]
+            gated = (mask * sigmoid(proj[width:]) * proj[:width]).astype(jnp.bfloat16)
+            outbox[:, at] = gated.reshape(owners, 2 * per, tokens)
+            return carry
+
+        lax.fori_loop(0, step_rows, one_row, 0)
+        fwd_own(chunk).start()
+
+        def send(step, carry):
+            fwd_copy(chunk, (me + step) % owners, me).start()
+            return carry
+
+        lax.fori_loop(1, owners, send, 0)
+
+    def contract(update):
+        def widen(chunk, source):
+            first = source * rows + chunk * step_rows
+            block = inbox[pl.ds(first, step_rows)].astype(jnp.float32)
+            base = pl.multiple_of(first * (2 * per), 2 * per)
+            block = block.reshape(-1, tokens)
+            for tile in range(tiles):
+                wide[tile, pl.ds(base, step_rows * 2 * per), :] = block[
+                    :, tile * 128 : (tile + 1) * 128
+                ]
+
+        for chunk in range(CHUNKS):
+            fwd_own(chunk).wait()
+            widen(chunk, me)
+
+            def arrive(step, carry):
+                source = (me + owners - step) % owners
+                fwd_copy(chunk, me, source).wait_recv()
+                widen(chunk, source)
+                return carry
+
+            lax.fori_loop(1, owners, arrive, 0)
+
+        axis = 0 if update == 1 else 1
+
+        def channel(index, carry):
+            def pick(first):
+                pieces = [
+                    wide[tile, pl.ds(first, tokens, stride=2 * per), :].astype(jnp.bfloat16)
+                    for tile in range(tiles)
+                ]
+                return jnp.concatenate(pieces, axis=1)
+
+            left, right = pick(index), pick(per + index)
+            tri = lax.dot_general(
+                left, right, (((axis,), (axis,)), ((), ())), preferred_element_type=jnp.float32
+            )
+            for tile in range(tiles):
+                products[tile, pl.ds(index, tokens, stride=per), :] = tri[
+                    :, tile * 128 : (tile + 1) * 128
+                ]
+            return carry
+
+        lax.fori_loop(0, per, channel, 0)
+
+        def sent(chunk):
+            def one(step, carry):
+                fwd_copy(chunk, (me + step) % owners, me).wait_send()
+                return carry
+
+            lax.fori_loop(1, owners, one, 0)
+
+        for chunk in range(CHUNKS):
+
+            def pack(target):
+                base = pl.multiple_of((target * rows + chunk * step_rows) * per, back_rows)
+                block = jnp.concatenate(
+                    [products[tile, pl.ds(base, back_rows), :] for tile in range(tiles)], axis=1
+                )
+                back_out[target, pl.ds(chunk * back_rows, back_rows)] = block.astype(jnp.bfloat16)
+
+            def give(step, carry):
+                target = (me + step) % owners
+                pack(target)
+                back_copy(chunk, target, me).start()
+                return carry
+
+            lax.fori_loop(1, owners, give, 0)
+            pack(me)
+            back_own(chunk).start()
+        for chunk in range(CHUNKS):
+            sent(chunk)
+
+    def consume(update, chunk):
+        def arrive(step, carry):
+            back_copy(chunk, me, (me + owners - step) % owners).wait_recv()
+            return carry
+
+        lax.fori_loop(1, owners, arrive, 0)
+        back_own(chunk).wait()
+
+        def two_rows(step, carry):
+            base = pl.multiple_of(chunk * back_rows + step * (2 * per), 2 * per)
+            both = back_in[:, pl.ds(base, 2 * per), :].astype(jnp.float32)
+            for which in range(2):
+                at = chunk * step_rows + 2 * step + which
+                tri = both[:, which * per : (which + 1) * per].reshape(owners * per, tokens)
+                flat_tri = normalise(tri, 0)
+                change = lax.dot_general(
+                    flat_tri,
+                    outw_v[update],
+                    (((0,), (0,)), ((), ())),
+                    preferred_element_type=jnp.float32,
+                )
+                gating = sigmoid(
+                    jnp.dot(normed[at], gate_v[update], preferred_element_type=jnp.float32)
+                )
+                values = cells[at].astype(jnp.float32) + gating * change
+                cells[at] = values.astype(jnp.bfloat16)
+            return carry
+
+        lax.fori_loop(0, step_rows // 2, two_rows, 0)
+
+    def returned():
+        for chunk in range(CHUNKS):
+
+            def one(step, carry):
+                back_copy(chunk, (me + step) % owners, me).wait_send()
+                return carry
+
+            lax.fori_loop(1, owners, one, 0)
+
+    def results(chunk):
+        at = pl.ds(chunk * step_rows, step_rows)
+        to = pl.ds(col * rows + chunk * step_rows, step_rows)
+        own = pltpu.make_async_copy(
+            cells.at[at, pl.ds(mine, half)], out_ref.at[to], out_sems.at[0, chunk]
+        )
+        other = pltpu.make_async_remote_copy(
+            src_ref=cells.at[at, pl.ds(theirs, half)],
+            dst_ref=out_ref.at[to],
+            send_sem=out_sems.at[1, chunk],
+            recv_sem=out_sems.at[2, chunk],
+            device_id=sibling,
+            device_id_type=MESH,
+        )
+        return own, other
+
+    for chunk in range(CHUNKS):
+        produce(0, chunk)
+    contract(0)
+    for chunk in range(CHUNKS):
+        consume(0, chunk)
+        produce(1, chunk)
+    returned()
+    contract(1)
+    for chunk in range(CHUNKS):
+        consume(1, chunk)
+        for copy in results(chunk):
+            copy.start()
+    returned()
+    for chunk in range(CHUNKS):
+        for copy in results(chunk):
+            copy.wait()
+
+
+def fused_shards(
+    pair, chain_ids, token_mask, same_chain_bias, proj_weight, gate_weight, out_weight
+):
+    rows_tile, cols_tile, channels = pair.shape
+    rows_grid = lax.axis_size("row")
+    owners = 2 * rows_grid
+    tokens = 2 * cols_tile
+    rows = rows_tile // 2
+    hidden = proj_weight.shape[2] // 4
+    per = hidden // owners
+    parts = proj_weight.reshape(2, channels, 2, 2, owners, per)
+    proj = parts.transpose(0, 3, 4, 2, 5, 1).reshape(2, 4 * hidden, channels)
+    chain_cols = jnp.broadcast_to(chain_ids[:, None], (tokens, channels))
+    mask = token_mask.astype(jnp.float32)
+    bf16, f32 = jnp.bfloat16, jnp.float32
+    vmem = pl.BlockSpec(memory_space=pltpu.VMEM)
+    smem = pl.BlockSpec(memory_space=pltpu.SMEM)
+    anywhere = pl.BlockSpec(memory_space=pl.ANY)
+    return pl.pallas_call(
+        functools.partial(fused_kernel, rows_grid),
+        out_shape=jax.ShapeDtypeStruct(pair.shape, pair.dtype),
+        in_specs=[anywhere, smem, smem, vmem, vmem, vmem, vmem, vmem, vmem],
+        out_specs=anywhere,
+        scratch_shapes=[
+            pltpu.VMEM((rows, tokens, channels), bf16),
+            pltpu.VMEM((rows, tokens, channels), bf16),
+            pltpu.VMEM((owners, rows, 2 * per, tokens), bf16),
+            pltpu.VMEM((tokens, 2 * per, tokens), bf16),
+            pltpu.VMEM((tokens // 128, tokens * 2 * per, 128), f32),
+            pltpu.VMEM((tokens // 128, tokens * per, 128), f32),
+            pltpu.VMEM((owners, rows * per, tokens), bf16),
+            pltpu.VMEM((owners, rows * per, tokens), bf16),
+            pltpu.SemaphoreType.DMA((3,)),
+            pltpu.SemaphoreType.DMA((CHUNKS, owners)),
+            pltpu.SemaphoreType.DMA((CHUNKS, owners)),
+            pltpu.SemaphoreType.DMA((CHUNKS, owners)),
+            pltpu.SemaphoreType.DMA((CHUNKS, owners)),
+            pltpu.SemaphoreType.DMA((2, CHUNKS)),
+            pltpu.SemaphoreType.DMA((3, CHUNKS)),
+        ],
+        compiler_params=pltpu.CompilerParams(
+            collective_id=0, has_side_effects=True, vmem_limit_bytes=56 * 1024 * 1024
+        ),
+    )(
+        pair,
+        chain_ids,
+        mask,
+        chain_cols,
+        mask[None, :],
+        same_chain_bias.astype(f32)[None, :],
+        proj,
+        gate_weight,
+        out_weight,
+    )
+
+
+def fits(pair, proj_weight):
+    rows_tile, cols_tile, channels = pair.shape
+    rows_grid, cols_grid = lax.axis_size("row"), lax.axis_size("col")
+    hidden = proj_weight.shape[2] // 4
+    return (
+        cols_grid == 2
+        and hidden == 8 * cols_grid * rows_grid
+        and channels == 128
+        and rows_tile % (4 * CHUNKS) == 0
+        and cols_tile % 64 == 0
+        and (2 * cols_tile) % 128 == 0
+        and rows_tile * rows_grid == cols_tile * cols_grid
+    )
+
+
+def program_shards(pair, chain_ids, token_mask, same_chain_bias, proj_weight, *rest):
+    chosen = fused_shards if fits(pair, proj_weight) else shards
+    return chosen(pair, chain_ids, token_mask, same_chain_bias, proj_weight, *rest)
+
+
 def solution(mesh):
     return jax.shard_map(
-        shards,
+        program_shards,
         mesh=mesh,
         in_specs=(P(("group", "row"), "col", None), P("group"), P("group"), P(), P(), P(), P()),
         out_specs=P(("group", "row"), "col", None),

time: 540 us -> 336 us (0.62); the launches traced: 533 us -> 335 us
  Pallas kernels: 0 us -> 326 us
  blocking collectives: 219 us -> 0 us
  local copies, waits for them, and re-layouts: 128 us -> 7.14 us
  waiting for transfers between devices: 94.2 us -> 0 us
  matrix products: 39.5 us -> 0 us
  other arithmetic: 40.3 us -> 1.92 us
  starting transfers between devices: 10.9 us -> 0 us
    pallas_call x0 -> x1, Pallas kernels: none -> 326 us  [fused_shards(): pl.pallas_call(functools.partial(fused_kernel, rows_grid), out_shape=jax....]
    all_to_all x2 -> x0, blocking collectives: 219 us -> none  [triangle(): lax.all_to_all(stacked, ('row', 'col'), split_axis=0, concat_axis=0, tile...]
    all_to_all x2 -> x0, waiting for transfers between devices: 94.2 us -> none  [triangle(): lax.all_to_all(result, ('row', 'col'), split_axis=0, concat_axis=0, tiled...]
    reshape x10 -> x0, local copies, waits for them, and re-layouts: 76.4 us -> none  [the longest x4 45.3 us: contract(): whole = pieces.reshape(rows_grid, cols_grid, 2, items, rows_tile, cols_tile)]
    dot_general x8 -> x0, matrix products: 39.5 us -> none  [the longest x2 11.8 us: triangle(): jnp.dot(normed, gate, preferred_element_type=jnp.float32)]
    squeeze x4 -> x0, local copies, waits for them, and re-layouts: 20.6 us -> none  [the longest x2 14.8 us: contract(): whole[0]]
    convert_element_type x7 -> x1, other arithmetic: 19.1 us -> 0.68 us  [fused_shards(): mask = token_mask.astype(jnp.float32)]
    reduce_sum x7 -> x0, other arithmetic: 15.5 us -> none  [the longest x4 10.3 us: layer_norm(): var = jnp.mean(centred * centred, axis=-1, keepdims=True)]
  transfers between devices with their start and end apart: 2 -> 0, of which waited for: 2 -> 0; matrix products, arithmetic and copies ran while one was open for 2% -> 0% of each run, Pallas kernels for 0% -> 0%
where the time goes in v1:
time: 336 us; the launch traced here: 335 us
  Pallas kernels  326 us (97%)
  local copies, waits for them, and re-layouts  7.14 us (2%)
    pallas_call x1, Pallas kernels, fused_shards(): pl.pallas_call(functools.partial(fused_kernel, rows_grid), out_shape=jax....  326 us

profile of v1, /device:TPU:15, one launch (start us, length us, event | category | flops | bytes accessed | tf_op | source)
XLA Modules:
  0.0 335.0 jit_solution(6359679365486597882)
XLA Ops:
  0.0 1.2 bitcast_convert_fusion.bias_v
  1.2 0.7 convert_element_type.4.mask_s
  1.9 0.0 copy-start
  1.9 0.6 broadcast_in_dim.15.mask_v
  2.5 1.5 broadcast_in_dim.14.chain_v
  4.0 1.1 copy.9
  5.1 0.8 copy.10
  5.8 0.0 copy-done
  5.8 326.0 %shard_map.73 = bf16[48,192,128]{2,1,0:T(8,128)(2,1)} custom-call(bf16[48,192,128]{2,1,0:T(8,128)(2,1)} %pair_ref.1, s32[384]{0:T(512)} %chain_s.1, f32[384]{0:T(512)} %copy-done, s32[384,128]{1,0:T(8,128)} %broadcast_in_dim.14.chain_v, f32[1,384]{1,0:T(1,128)} %broadcast_in_dim.15.mask_v, f32[1,128]{1,0:T(1,128)} %bitcast_convert_fusion.bias_v, ...), custom_call_target="tpu_custom_call" | custom-call | tf_op jit(solution)/shard_map/pallas_call | solution.py:407
  331.8 3.2 copy.12
Async XLA Ops:
  1.9 3.9 %copy-start = (f32[384]{0:T(512)}, f32[384]{0:T(512)S(1)}, u32[]{:S(2)}) copy-start(f32[384]{0:T(512)S(1)} %convert_element_type.4.mask_s) | copy-start | bytes 4612

commit v2 on v1

--- a/solution.py
+++ b/solution.py
@@ -116,12 +116,18 @@
     cells,
     normed,
     outbox,
+    left_in,
+    right_in,
     inbox,
     wide,
     products,
     back_out,
     back_in,
     pair_sems,
+    left_send,
+    left_recv,
+    right_send,
+    right_recv,
     fwd_send,
     fwd_recv,
     back_send,
@@ -130,13 +136,18 @@
     out_sems,
 ):
     owners = 2 * rows_grid
+    team = owners // 2
     rows, tokens, _ = cells.shape
     half = tokens // 2
     per = inbox.shape[1] // 2
+    wide_per = 2 * per
     step_rows = rows // CHUNKS
     tiles = tokens // 128
     row, col = lax.axis_index("row"), lax.axis_index("col")
     me = row * 2 + col
+    seat = me % team
+    base_team = me - seat
+    other_team = team - base_team
     sibling = {"row": row, "col": 1 - col}
     mine = pl.multiple_of(col * half, half)
     theirs = pl.multiple_of((1 - col) * half, half)
@@ -171,9 +182,49 @@
     keep.wait()
     swap.wait()
 
+    def part(chunk):
+        return pl.ds(chunk * step_rows, step_rows)
+
+    def left_copy(chunk, target, source):
+        return pltpu.make_async_remote_copy(
+            src_ref=outbox.at[target, part(chunk), pl.ds(0, wide_per)],
+            dst_ref=left_in.at[pl.ds(source * rows + chunk * step_rows, step_rows)],
+            send_sem=left_send.at[chunk, target],
+            recv_sem=left_recv.at[chunk, source],
+            device_id=place(base_team + target),
+            device_id_type=MESH,
+        )
+
+    def left_own(chunk):
+        return pltpu.make_async_copy(
+            outbox.at[seat, part(chunk), pl.ds(0, wide_per)],
+            left_in.at[pl.ds(seat * rows + chunk * step_rows, step_rows)],
+            own_sems.at[0, chunk],
+        )
+
+    def right_copy(chunk, target, source):
+        return pltpu.make_async_remote_copy(
+            src_ref=outbox.at[target % team, part(chunk), pl.ds(wide_per, wide_per)],
+            dst_ref=right_in.at[pl.ds(source * rows + chunk * step_rows, step_rows)],
+            send_sem=right_send.at[chunk, target],
+            recv_sem=right_recv.at[chunk, source],
+            device_id=place(target),
+            device_id_type=MESH,
+        )
+
+    def right_own(chunk):
+        return pltpu.make_async_copy(
+            outbox.at[seat, part(chunk), pl.ds(wide_per, wide_per)],
+            right_in.at[pl.ds(me * rows + chunk * step_rows, step_rows)],
+            own_sems.at[1, chunk],
+        )
+
+    def share(owner):
+        return pl.ds(pl.multiple_of((owner % 2) * wide_per, wide_per), wide_per)
+
     def fwd_copy(chunk, owner, source):
         return pltpu.make_async_remote_copy(
-            src_ref=outbox.at[owner, pl.ds(chunk * step_rows, step_rows)],
+            src_ref=outbox.at[owner // 2, part(chunk), share(owner)],
             dst_ref=inbox.at[pl.ds(source * rows + chunk * step_rows, step_rows)],
             send_sem=fwd_send.at[chunk, owner],
             recv_sem=fwd_recv.at[chunk, source],
@@ -183,34 +234,77 @@
 
     def fwd_own(chunk):
         return pltpu.make_async_copy(
-            outbox.at[me, pl.ds(chunk * step_rows, step_rows)],
+            outbox.at[me // 2, part(chunk), share(me)],
             inbox.at[pl.ds(me * rows + chunk * step_rows, step_rows)],
-            own_sems.at[0, chunk],
-        )
-
-    back_rows = step_rows * per
-
-    def back_copy(chunk, target, source):
+            own_sems.at[2, chunk],
+        )
+
+    def back_view(ref, update, chunk, owner):
+        if update == 0:
+            size = step_rows * wide_per
+            return ref.at[owner, pl.ds(chunk * size, size)]
+        size = step_rows * per
+        first = pl.multiple_of((owner % 2) * (rows * per) + chunk * size, size)
+        return ref.at[owner // 2, pl.ds(first, size)]
+
+    def back_copy(update, chunk, target, source):
         return pltpu.make_async_remote_copy(
-            src_ref=back_out.at[target, pl.ds(chunk * back_rows, back_rows)],
-            dst_ref=back_in.at[source, pl.ds(chunk * back_rows, back_rows)],
+            src_ref=back_view(back_out, update, chunk, target),
+            dst_ref=back_view(back_in, update, chunk, source),
             send_sem=back_send.at[chunk, target],
             recv_sem=back_recv.at[chunk, source],
-            device_id=place(target),
+            device_id=place(target + base_team if update == 0 else target),
             device_id_type=MESH,
         )
 
-    def back_own(chunk):
+    def back_own(update, chunk):
+        at = seat if update == 0 else me
         return pltpu.make_async_copy(
-            back_out.at[me, pl.ds(chunk * back_rows, back_rows)],
-            back_in.at[me, pl.ds(chunk * back_rows, back_rows)],
-            own_sems.at[1, chunk],
-        )
+            back_view(back_out, update, chunk, at),
+            back_view(back_in, update, chunk, at),
+            own_sems.at[3, chunk],
+        )
+
+    def each(first, last, act):
+        def body(step, carry):
+            act(step)
+            return carry
+
+        lax.fori_loop(first, last, body, 0)
+
+    def send_first(chunk):
+        def act(step):
+            near = (seat + step) % team
+            right_copy(chunk, other_team + near, me).start()
+            right_copy(chunk, base_team + near, me).start()
+            left_copy(chunk, near, seat).start()
+
+        left_own(chunk).start()
+        right_own(chunk).start()
+        right_copy(chunk, other_team + seat, me).start()
+        each(1, team, act)
+
+    def sent_first(chunk):
+        def act(step):
+            near = (seat + step) % team
+            right_copy(chunk, other_team + near, me).wait_send()
+            right_copy(chunk, base_team + near, me).wait_send()
+            left_copy(chunk, near, seat).wait_send()
+
+        right_copy(chunk, other_team + seat, me).wait_send()
+        each(1, team, act)
+
+    def send_second(chunk):
+        fwd_own(chunk).start()
+        each(1, owners, lambda step: fwd_copy(chunk, (me + step) % owners, me).start())
+
+    def sent_second(chunk):
+        each(1, owners, lambda step: fwd_copy(chunk, (me + step) % owners, me).wait_send())
 
     def produce(update, chunk):
-        def one_row(step, carry):
+        def one_row(step):
             at = chunk * step_rows + step
-            token = row * (2 * rows) + col * rows + at
+            token = me * rows + at
             values = cells[at].astype(jnp.float32)
             if update == 0:
                 same = chain_v[...] == chain_s[token]
@@ -228,132 +322,171 @@
             width = proj.shape[0] // 2
             mask = mask_s[token] * mask_v[...]
             gated = (mask * sigmoid(proj[width:]) * proj[:width]).astype(jnp.bfloat16)
-            outbox[:, at] = gated.reshape(owners, 2 * per, tokens)
-            return carry
-
-        lax.fori_loop(0, step_rows, one_row, 0)
-        fwd_own(chunk).start()
-
-        def send(step, carry):
-            fwd_copy(chunk, (me + step) % owners, me).start()
-            return carry
-
-        lax.fori_loop(1, owners, send, 0)
-
-    def contract(update):
-        def widen(chunk, source):
-            first = source * rows + chunk * step_rows
-            block = inbox[pl.ds(first, step_rows)].astype(jnp.float32)
-            base = pl.multiple_of(first * (2 * per), 2 * per)
-            block = block.reshape(-1, tokens)
-            for tile in range(tiles):
-                wide[tile, pl.ds(base, step_rows * 2 * per), :] = block[
-                    :, tile * 128 : (tile + 1) * 128
-                ]
-
+            outbox[:, at] = gated.reshape(team, 2 * wide_per, tokens)
+
+        each(0, step_rows, one_row)
+        if update == 0:
+            send_first(chunk)
+        else:
+            send_second(chunk)
+
+    def widen(box, chunk, source, offset):
+        first = source * rows + chunk * step_rows
+        block = box[pl.ds(first, step_rows)].astype(jnp.float32).reshape(-1, tokens)
+        base = pl.multiple_of(offset + first * wide_per, wide_per)
+        for tile in range(tiles):
+            wide[tile, pl.ds(base, step_rows * wide_per), :] = block[
+                :, tile * 128 : (tile + 1) * 128
+            ]
+
+    def pick(first, size):
+        pieces = [
+            wide[tile, pl.ds(first, size, stride=wide_per), :].astype(jnp.bfloat16)
+            for tile in range(tiles)
+        ]
+        return jnp.concatenate(pieces, axis=1)
+
+    def keep_product(tri, index, count):
+        size = tri.shape[0]
+        for tile in range(tiles):
+            products[tile, pl.ds(index, size, stride=count), :] = tri[
+                :, tile * 128 : (tile + 1) * 128
+            ]
+
+    def give_back(update, count, people, own):
+        for chunk in range(CHUNKS):
+            size = step_rows * count
+
+            def pack(target):
+                base = pl.multiple_of((target * rows + chunk * step_rows) * count, size)
+                block = jnp.concatenate(
+                    [products[tile, pl.ds(base, size), :] for tile in range(tiles)], axis=1
+                )
+                back_view(back_out, update, chunk, target)[...] = block.astype(jnp.bfloat16)
+
+            def give(step):
+                target = (own + step) % people
+                pack(target)
+                back_copy(update, chunk, target, own).start()
+
+            each(1, people, give)
+            pack(own)
+            back_own(update, chunk).start()
+
+    def contract_first():
+        team_rows = team * rows
+        offset = team_rows * wide_per
+        for chunk in range(CHUNKS):
+            left_own(chunk).wait()
+            right_own(chunk).wait()
+            widen(left_in, chunk, seat, 0)
+            widen(right_in, chunk, me, offset)
+
+            def arrive(step):
+                near = (seat + team - step) % team
+                right_copy(chunk, me, other_team + near).wait_recv()
+                widen(right_in, chunk, other_team + near, offset)
+                right_copy(chunk, me, base_team + near).wait_recv()
+                widen(right_in, chunk, base_team + near, offset)
+                left_copy(chunk, seat, near).wait_recv()
+                widen(left_in, chunk, near, 0)
+
+            right_copy(chunk, me, other_team + seat).wait_recv()
+            widen(right_in, chunk, other_team + seat, offset)
+            each(1, team, arrive)
+
+        def channel(index):
+            left = pick(index, team_rows)
+            right = pick(offset + index, tokens)
+            tri = lax.dot_general(
+                left, right, (((1,), (1,)), ((), ())), preferred_element_type=jnp.float32
+            )
+            keep_product(tri, index, wide_per)
+
+        each(0, wide_per, channel)
+        give_back(0, wide_per, team, seat)
+        for chunk in range(CHUNKS):
+            sent_first(chunk)
+
+    def contract_second():
         for chunk in range(CHUNKS):
             fwd_own(chunk).wait()
-            widen(chunk, me)
-
-            def arrive(step, carry):
+            widen(inbox, chunk, me, 0)
+
+            def arrive(step):
                 source = (me + owners - step) % owners
                 fwd_copy(chunk, me, source).wait_recv()
-                widen(chunk, source)
-                return carry
-
-            lax.fori_loop(1, owners, arrive, 0)
-
-        axis = 0 if update == 1 else 1
-
-        def channel(index, carry):
-            def pick(first):
-                pieces = [
-                    wide[tile, pl.ds(first, tokens, stride=2 * per), :].astype(jnp.bfloat16)
-                    for tile in range(tiles)
-                ]
-                return jnp.concatenate(pieces, axis=1)
-
-            left, right = pick(index), pick(per + index)
+                widen(inbox, chunk, source, 0)
+
+            each(1, owners, arrive)
+
+        def channel(index):
+            left = pick(index, tokens)
+            right = pick(per + index, tokens)
             tri = lax.dot_general(
-                left, right, (((axis,), (axis,)), ((), ())), preferred_element_type=jnp.float32
+                left, right, (((0,), (0,)), ((), ())), preferred_element_type=jnp.float32
             )
-            for tile in range(tiles):
-                products[tile, pl.ds(index, tokens, stride=per), :] = tri[
-                    :, tile * 128 : (tile + 1) * 128
-                ]
-            return carry
-
-        lax.fori_loop(0, per, channel, 0)
-
-        def sent(chunk):
-            def one(step, carry):
-                fwd_copy(chunk, (me + step) % owners, me).wait_send()
-                return carry
-
-            lax.fori_loop(1, owners, one, 0)
-
+            keep_product(tri, index, per)
+
+        each(0, per, channel)
+        give_back(1, per, owners, me)
         for chunk in range(CHUNKS):
-
-            def pack(target):
-                base = pl.multiple_of((target * rows + chunk * step_rows) * per, back_rows)
-                block = jnp.concatenate(
-                    [products[tile, pl.ds(base, back_rows), :] for tile in range(tiles)], axis=1
-                )
-                back_out[target, pl.ds(chunk * back_rows, back_rows)] = block.astype(jnp.bfloat16)
-
-            def give(step, carry):
-                target = (me + step) % owners
-                pack(target)
-                back_copy(chunk, target, me).start()
-                return carry
-
-            lax.fori_loop(1, owners, give, 0)
-            pack(me)
-            back_own(chunk).start()
+            sent_second(chunk)
+
+    def finish(update, at, tri):
+        flat_tri = normalise(tri, 0)
+        change = lax.dot_general(
+            flat_tri, outw_v[update], (((0,), (0,)), ((), ())), preferred_element_type=jnp.float32
+        )
+        gating = sigmoid(jnp.dot(normed[at], gate_v[update], preferred_element_type=jnp.float32))
+        cells[at] = (cells[at].astype(jnp.float32) + gating * change).astype(jnp.bfloat16)
+
+    def consume_first(chunk):
+        each(
+            1,
+            team,
+            lambda step: back_copy(0, chunk, seat, (seat + team - step) % team).wait_recv(),
+        )
+        back_own(0, chunk).wait()
+
+        def one_row(step):
+            at = chunk * step_rows + step
+            base = pl.multiple_of(at * wide_per, wide_per)
+            tri = back_in[:, pl.ds(base, wide_per), :].astype(jnp.float32)
+            finish(0, at, tri.reshape(owners * per, tokens))
+
+        each(0, step_rows, one_row)
+
+    def consume_second(chunk):
+        each(
+            1,
+            owners,
+            lambda step: back_copy(1, chunk, me, (me + owners - step) % owners).wait_recv(),
+        )
+        back_own(1, chunk).wait()
+
+        def two_rows(step):
+            at = chunk * step_rows + 2 * step
+            base = pl.multiple_of(at * per, wide_per)
+            even = back_in[:, pl.ds(base, wide_per), :].astype(jnp.float32)
+            odd = back_in[:, pl.ds(rows * per + base, wide_per), :].astype(jnp.float32)
+            for which in range(2):
+                lanes = slice(which * per, (which + 1) * per)
+                tri = jnp.concatenate([even[:, lanes], odd[:, lanes]], axis=1)
+                finish(1, at + which, tri.reshape(owners * per, tokens))
+
+        each(0, step_rows // 2, two_rows)
+
+    def returned(update, people, own):
         for chunk in range(CHUNKS):
-            sent(chunk)
-
-    def consume(update, chunk):
-        def arrive(step, carry):
-            back_copy(chunk, me, (me + owners - step) % owners).wait_recv()
-            return carry
-
-        lax.fori_loop(1, owners, arrive, 0)
-        back_own(chunk).wait()
-
-        def two_rows(step, carry):
-            base = pl.multiple_of(chunk * back_rows + step * (2 * per), 2 * per)
-            both = back_in[:, pl.ds(base, 2 * per), :].astype(jnp.float32)
-            for which in range(2):
-                at = chunk * step_rows + 2 * step + which
-                tri = both[:, which * per : (which + 1) * per].reshape(owners * per, tokens)
-                flat_tri = normalise(tri, 0)
-                change = lax.dot_general(
-                    flat_tri,
-                    outw_v[update],
-                    (((0,), (0,)), ((), ())),
-                    preferred_element_type=jnp.float32,
-                )
-                gating = sigmoid(
-                    jnp.dot(normed[at], gate_v[update], preferred_element_type=jnp.float32)
-                )
-                values = cells[at].astype(jnp.float32) + gating * change
-                cells[at] = values.astype(jnp.bfloat16)
-            return carry
-
-        lax.fori_loop(0, step_rows // 2, two_rows, 0)
-
-    def returned():
-        for chunk in range(CHUNKS):
-
-            def one(step, carry):
-                back_copy(chunk, (me + step) % owners, me).wait_send()
-                return carry
-
-            lax.fori_loop(1, owners, one, 0)
+            each(
+                1,
+                people,
+                lambda step: back_copy(update, chunk, (own + step) % people, own).wait_send(),
+            )
 
     def results(chunk):
-        at = pl.ds(chunk * step_rows, step_rows)
+        at = part(chunk)
         to = pl.ds(col * rows + chunk * step_rows, step_rows)
         own = pltpu.make_async_copy(
             cells.at[at, pl.ds(mine, half)], out_ref.at[to], out_sems.at[0, chunk]
@@ -370,20 +503,26 @@
 
     for chunk in range(CHUNKS):
         produce(0, chunk)
-    contract(0)
+    contract_first()
     for chunk in range(CHUNKS):
-        consume(0, chunk)
+        consume_first(chunk)
         produce(1, chunk)
-    returned()
-    contract(1)
+    returned(0, team, seat)
+    contract_second()
     for chunk in range(CHUNKS):
-        consume(1, chunk)
+        consume_second(chunk)
         for copy in results(chunk):
             copy.start()
-    returned()
+    returned(1, owners, me)
     for chunk in range(CHUNKS):
         for copy in results(chunk):
             copy.wait()
+
+
+def arrange(weight, groups):
+    channels, width = weight.shape
+    parts = weight.reshape(channels, 2, 2, groups, width // (4 * groups))
+    return parts.transpose(2, 3, 1, 4, 0).reshape(width, channels)
 
 
 def fused_shards(
@@ -392,18 +531,22 @@
     rows_tile, cols_tile, channels = pair.shape
     rows_grid = lax.axis_size("row")
     owners = 2 * rows_grid
+    team = owners // 2
     tokens = 2 * cols_tile
     rows = rows_tile // 2
     hidden = proj_weight.shape[2] // 4
     per = hidden // owners
-    parts = proj_weight.reshape(2, channels, 2, 2, owners, per)
-    proj = parts.transpose(0, 3, 4, 2, 5, 1).reshape(2, 4 * hidden, channels)
+    proj = jnp.stack([arrange(proj_weight[0], team), arrange(proj_weight[1], owners)])
     chain_cols = jnp.broadcast_to(chain_ids[:, None], (tokens, channels))
     mask = token_mask.astype(jnp.float32)
     bf16, f32 = jnp.bfloat16, jnp.float32
     vmem = pl.BlockSpec(memory_space=pltpu.VMEM)
     smem = pl.BlockSpec(memory_space=pltpu.SMEM)
     anywhere = pl.BlockSpec(memory_space=pl.ANY)
+
+    def sems(*shape):
+        return pltpu.SemaphoreType.DMA(shape)
+
     return pl.pallas_call(
         functools.partial(fused_kernel, rows_grid),
         out_shape=jax.ShapeDtypeStruct(pair.shape, pair.dtype),
@@ -412,22 +555,28 @@
         scratch_shapes=[
             pltpu.VMEM((rows, tokens, channels), bf16),
             pltpu.VMEM((rows, tokens, channels), bf16),
-            pltpu.VMEM((owners, rows, 2 * per, tokens), bf16),
+            pltpu.VMEM((team, rows, 4 * per, tokens), bf16),
+            pltpu.VMEM((team * rows, 2 * per, tokens), bf16),
             pltpu.VMEM((tokens, 2 * per, tokens), bf16),
-            pltpu.VMEM((tokens // 128, tokens * 2 * per, 128), f32),
+            pltpu.VMEM((tokens, 2 * per, tokens), bf16),
+            pltpu.VMEM((tokens // 128, (tokens + team * rows) * 2 * per, 128), f32),
             pltpu.VMEM((tokens // 128, tokens * per, 128), f32),
-            pltpu.VMEM((owners, rows * per, tokens), bf16),
-            pltpu.VMEM((owners, rows * per, tokens), bf16),
-            pltpu.SemaphoreType.DMA((3,)),
-            pltpu.SemaphoreType.DMA((CHUNKS, owners)),
-            pltpu.SemaphoreType.DMA((CHUNKS, owners)),
-            pltpu.SemaphoreType.DMA((CHUNKS, owners)),
-            pltpu.SemaphoreType.DMA((CHUNKS, owners)),
-            pltpu.SemaphoreType.DMA((2, CHUNKS)),
-            pltpu.SemaphoreType.DMA((3, CHUNKS)),
+            pltpu.VMEM((team, rows * 2 * per, tokens), bf16),
+            pltpu.VMEM((team, rows * 2 * per, tokens), bf16),
+            sems(3),
+            sems(CHUNKS, team),
+            sems(CHUNKS, team),
+            sems(CHUNKS, owners),
+            sems(CHUNKS, owners),
+            sems(CHUNKS, owners),
+            sems(CHUNKS, owners),
+            sems(CHUNKS, owners),
+            sems(CHUNKS, owners),
+            sems(4, CHUNKS),
+            sems(3, CHUNKS),
         ],
         compiler_params=pltpu.CompilerParams(
-            collective_id=0, has_side_effects=True, vmem_limit_bytes=56 * 1024 * 1024
+            collective_id=0, has_side_effects=True, vmem_limit_bytes=60 * 1024 * 1024
         ),
     )(
         pair,
@@ -448,6 +597,7 @@
     hidden = proj_weight.shape[2] // 4
     return (
         cols_grid == 2
+        and rows_grid % 2 == 0
         and hidden == 8 * cols_grid * rows_grid
         and channels == 128
         and rows_tile % (4 * CHUNKS) == 0

time: 336 us -> 317 us (0.943)
  Pallas kernels: 326 us -> 304 us
    pallas_call x1, Pallas kernels: 326 us -> 304 us  [fused_shards(): pl.pallas_call(functools.partial(fused_kernel, rows_grid), out_shape=jax....]
where the time goes in v2:
time: 317 us; the launch traced here: 314 us
  Pallas kernels  304 us (96%)
  local copies, waits for them, and re-layouts  6.55 us (2%)
    pallas_call x1, Pallas kernels, fused_shards(): pl.pallas_call(functools.partial(fused_kernel, rows_grid), out_shape=jax....  304 us

profile of v2, /device:TPU:15, one launch (start us, length us, event | category | flops | bytes accessed | tf_op | source)
XLA Modules:
  0.0 313.7 jit_solution(7885764692625262975)
XLA Ops:
  0.0 1.2 bitcast_convert_fusion.bias_v
  1.2 0.7 convert_element_type.4.mask_s
  1.9 0.0 copy-start
  1.9 0.6 broadcast_in_dim.15.mask_v
  2.5 1.5 broadcast_in_dim.14.chain_v
  3.9 1.0 fusion
  4.9 0.1 copy.14
  5.1 0.1 copy.15
  5.2 0.7 pad_maximum_fusion.proj_v
  5.9 0.0 copy-done
  5.9 304.5 %shard_map.73 = bf16[48,192,128]{2,1,0:T(8,128)(2,1)} custom-call(bf16[48,192,128]{2,1,0:T(8,128)(2,1)} %pair_ref.1, s32[384]{0:T(512)} %chain_s.1, f32[384]{0:T(512)} %copy-done, s32[384,128]{1,0:T(8,128)} %broadcast_in_dim.14.chain_v, f32[1,384]{1,0:T(1,128)} %broadcast_in_dim.15.mask_v, f32[1,128]{1,0:T(1,128)} %bitcast_convert_fusion.bias_v, ...), custom_call_target="tpu_custom_call" | custom-call | tf_op jit(solution)/shard_map/pallas_call | solution.py:550
  310.4 3.2 %copy.17 = bf16[48,192,128]{2,1,0:T(8,128)(2,1)} copy(bf16[48,192,128]{2,1,0:T(8,128)(2,1)} %shard_map.73) | data formatting | bytes 4718592
  (2 shorter events, 0.0 us)
Async XLA Ops:
  1.9 4.1 %copy-start = (f32[384]{0:T(512)}, f32[384]{0:T(512)S(1)}, u32[]{:S(2)}) copy-start(f32[384]{0:T(512)S(1)} %convert_element_type.4.mask_s) | copy-start | bytes 4612

commit v3 on v0

--- a/solution.py
+++ b/solution.py
@@ -1,7 +1,14 @@
+import functools
+
 import jax
 import jax.numpy as jnp
 from jax import lax
+from jax.experimental import pallas as pl
+from jax.experimental.pallas import tpu as pltpu
 from jax.sharding import PartitionSpec as P
+
+MESH = pl.DeviceIdType.MESH
+CHUNKS = 3
 
 
 def layer_norm(values):
@@ -83,9 +90,616 @@
     return triangle(first, mask_flat, proj_weight[1], gate_weight[1], out_weight[1], True)
 
 
+def sigmoid(values):
+    return 0.5 * jnp.tanh(0.5 * values) + 0.5
+
+
+def normalise(values, axis):
+    mean = jnp.mean(values, axis=axis, keepdims=True)
+    centred = values - mean
+    var = jnp.mean(centred * centred, axis=axis, keepdims=True)
+    return (centred * lax.rsqrt(var + 1e-05)).astype(jnp.bfloat16)
+
+
+def fused_kernel(
+    rows_grid,
+    pair_ref,
+    chain_s,
+    mask_s,
+    chain_v,
+    mask_v,
+    bias_v,
+    proj_v,
+    gate_v,
+    outw_v,
+    out_ref,
+    cells,
+    normed,
+    first_out,
+    left_in,
+    right_in,
+    wide,
+    products,
+    back_out,
+    back_in,
+    second_out,
+    second_in,
+    others,
+    cross_out,
+    cross_in,
+    last_out,
+    last_in,
+    pair_sems,
+    left_send,
+    left_recv,
+    right_send,
+    right_recv,
+    back_send,
+    back_recv,
+    second_send,
+    second_recv,
+    cross_send,
+    cross_recv,
+    last_send,
+    last_recv,
+    own_sems,
+    last_own,
+    out_sems,
+):
+    owners = 2 * rows_grid
+    team = owners // 2
+    rows, tiles, chips, pair_rows, channels = cells.shape
+    step_rows = rows // CHUNKS
+    lanes = chips * pair_rows
+    tokens = tiles * lanes
+    per = left_in.shape[1]
+    team_rows = team * rows
+    batch = 4
+    row, col = lax.axis_index("row"), lax.axis_index("col")
+    me = row * 2 + col
+    seat = me % team
+    base_team = me - seat
+    other_team = team - base_team
+    sibling = {"row": row, "col": 1 - col}
+    half_chips = chips // 2
+
+    def place(owner):
+        return {"row": owner // 2, "col": owner % 2}
+
+    def each(first, last, act):
+        def body(step, carry):
+            act(step)
+            return carry
+
+        lax.fori_loop(first, last, body, 0)
+
+    barrier = pltpu.get_barrier_semaphore()
+
+    def greet(step):
+        pl.semaphore_signal(
+            barrier, inc=1, device_id=place((me + step) % owners), device_id_type=MESH
+        )
+
+    each(1, owners, greet)
+    pl.semaphore_wait(barrier, owners - 1)
+
+    def part(chunk):
+        return pl.ds(chunk * step_rows, step_rows)
+
+    def tile_rows(chunk, core):
+        return pl.ds(chunk * (2 * step_rows) + core * step_rows, step_rows)
+
+    def pair_copies(chunk, tile):
+        into = cells.at[part(chunk), tile, pl.ds(col * half_chips, half_chips)]
+        own = pltpu.make_async_copy(
+            pair_ref.at[tile_rows(chunk, col), :, tile], into, pair_sems.at[0, chunk, tile]
+        )
+        other = pltpu.make_async_remote_copy(
+            src_ref=pair_ref.at[tile_rows(chunk, 1 - col), :, tile],
+            dst_ref=into,
+            send_sem=pair_sems.at[1, chunk, tile],
+            recv_sem=pair_sems.at[2, chunk, tile],
+            device_id=sibling,
+            device_id_type=MESH,
+        )
+        return own, other
+
+    def out_copies(chunk, tile):
+        to = out_ref.at[tile_rows(chunk, col), :, tile]
+        own = pltpu.make_async_copy(
+            cells.at[part(chunk), tile, pl.ds(col * half_chips, half_chips)],
+            to,
+            out_sems.at[0, chunk, tile],
+        )
+        other = pltpu.make_async_remote_copy(
+            src_ref=cells.at[part(chunk), tile, pl.ds((1 - col) * half_chips, half_chips)],
+            dst_ref=to,
+            send_sem=out_sems.at[1, chunk, tile],
+            recv_sem=out_sems.at[2, chunk, tile],
+            device_id=sibling,
+            device_id_type=MESH,
+        )
+        return own, other
+
+    def left_copy(chunk, target, source):
+        return pltpu.make_async_remote_copy(
+            src_ref=first_out.at[target, part(chunk), pl.ds(0, per)],
+            dst_ref=left_in.at[pl.ds(source * rows + chunk * step_rows, step_rows)],
+            send_sem=left_send.at[chunk, target],
+            recv_sem=left_recv.at[chunk, source],
+            device_id=place(base_team + target),
+            device_id_type=MESH,
+        )
+
+    def left_own(chunk):
+        return pltpu.make_async_copy(
+            first_out.at[seat, part(chunk), pl.ds(0, per)],
+            left_in.at[pl.ds(seat * rows + chunk * step_rows, step_rows)],
+            own_sems.at[0, chunk],
+        )
+
+    def right_copy(chunk, target, source):
+        return pltpu.make_async_remote_copy(
+            src_ref=first_out.at[target % team, part(chunk), pl.ds(per, per)],
+            dst_ref=right_in.at[chunk, pl.ds(source * step_rows, step_rows)],
+            send_sem=right_send.at[chunk, target],
+            recv_sem=right_recv.at[chunk, source],
+            device_id=place(target),
+            device_id_type=MESH,
+        )
+
+    def right_own(chunk):
+        return pltpu.make_async_copy(
+            first_out.at[seat, part(chunk), pl.ds(per, per)],
+            right_in.at[chunk, pl.ds(me * step_rows, step_rows)],
+            own_sems.at[1, chunk],
+        )
+
+    def team_copy(out_box, in_box, send, recv, index, target, source):
+        return pltpu.make_async_remote_copy(
+            src_ref=out_box.at[index, target],
+            dst_ref=in_box.at[index, source],
+            send_sem=send.at[index, target],
+            recv_sem=recv.at[index, source],
+            device_id=place(base_team + target),
+            device_id_type=MESH,
+        )
+
+    back_copy = functools.partial(team_copy, back_out, back_in, back_send, back_recv)
+    second_copy = functools.partial(team_copy, second_out, second_in, second_send, second_recv)
+    last_copy = functools.partial(team_copy, last_out, last_in, last_send, last_recv)
+
+    def back_own(tile):
+        return pltpu.make_async_copy(
+            back_out.at[tile, seat], back_in.at[tile, seat], own_sems.at[2, tile]
+        )
+
+    def second_own(tile):
+        return pltpu.make_async_copy(
+            second_out.at[tile, seat], second_in.at[tile, seat], own_sems.at[3, tile]
+        )
+
+    def last_own_copy(block):
+        return pltpu.make_async_copy(
+            last_out.at[block, seat], last_in.at[block, seat], last_own.at[block]
+        )
+
+    def cross_copy(block):
+        return pltpu.make_async_remote_copy(
+            src_ref=cross_out.at[block],
+            dst_ref=cross_in.at[block],
+            send_sem=cross_send.at[block],
+            recv_sem=cross_recv.at[block],
+            device_id=place(other_team + seat),
+            device_id_type=MESH,
+        )
+
+    def near(step):
+        return (seat + step) % team
+
+    def send_left(chunk):
+        left_own(chunk).start()
+        each(1, team, lambda step: left_copy(chunk, near(step), seat).start())
+
+    def send_right(chunk):
+        def act(step):
+            right_copy(chunk, other_team + near(step), me).start()
+            right_copy(chunk, base_team + near(step), me).start()
+
+        right_own(chunk).start()
+        right_copy(chunk, other_team + seat, me).start()
+        each(1, team, act)
+
+    def project(update, flat):
+        proj = lax.dot_general(
+            proj_v[update], flat, (((1,), (1,)), ((), ())), preferred_element_type=jnp.float32
+        )
+        width = proj.shape[0] // 2
+        return sigmoid(proj[width:]) * proj[:width]
+
+    def mask_at(at):
+        chunk, step = at // step_rows, at % step_rows
+        return row * (2 * rows) + chunk * (2 * step_rows) + col * step_rows + step
+
+    def produce_first(chunk):
+        def one_row(step):
+            at = chunk * step_rows + step
+            token = mask_at(at)
+            values = cells[at].reshape(tokens, channels).astype(jnp.float32)
+            same = chain_v[...] == chain_s[token]
+            start = (values + jnp.where(same, bias_v[...], 0.0)).astype(jnp.bfloat16)
+            cells[at] = start.reshape(tiles, chips, pair_rows, channels)
+            flat = normalise(start.astype(jnp.float32), 1)
+            normed[at] = flat.reshape(tiles, lanes, channels)
+            gated = (mask_s[token] * mask_v[...]) * project(0, flat)
+            first_out[:, at] = gated.astype(jnp.bfloat16).reshape(team, 2 * per, tokens)
+
+        each(0, step_rows, one_row)
+
+    def widen(block, base):
+        block = block.astype(jnp.float32).reshape(-1, block.shape[-1])
+        size = block.shape[0]
+        for tile in range(block.shape[1] // lanes):
+            wide[tile, pl.ds(base, size), :] = block[:, tile * lanes : (tile + 1) * lanes]
+
+    def pick(first, size, stride):
+        pieces = [
+            wide[tile, pl.ds(first, size, stride=stride), :].astype(jnp.bfloat16)
+            for tile in range(tiles)
+        ]
+        return jnp.concatenate(pieces, axis=1)
+
+    right_base = team_rows * per
+
+    def widen_left(chunk, source):
+        first = source * rows + chunk * step_rows
+        widen(left_in[pl.ds(first, step_rows)], pl.multiple_of(first * per, per))
+
+    def widen_right(chunk, source):
+        first = source * step_rows
+        base = pl.multiple_of(right_base + first * per, per)
+        widen(right_in[chunk, pl.ds(first, step_rows)], base)
+
+    def take_left():
+        for chunk in range(CHUNKS):
+            left_own(chunk).wait()
+            widen_left(chunk, seat)
+
+            def arrive(step):
+                source = (seat + team - step) % team
+                left_copy(chunk, seat, source).wait_recv()
+                widen_left(chunk, source)
+
+            each(1, team, arrive)
+
+    def take_right(chunk):
+        def arrive(step):
+            source = (me + owners - step) % owners
+            right_copy(chunk, me, source).wait_recv()
+            widen_right(chunk, source)
+
+        right_own(chunk).wait()
+        widen_right(chunk, me)
+        each(1, owners, arrive)
+
+    def contract_first(tile):
+        def channel(index):
+            left = pick(index, team_rows, per)
+            right = pick(right_base + index, lanes, per)
+            tri = lax.dot_general(
+                left, right, (((1,), (1,)), ((), ())), preferred_element_type=jnp.float32
+            )
+            products[pl.ds(index, team_rows, stride=per), :] = tri
+
+        each(0, per, channel)
+        size = rows * per
+
+        def give(step):
+            target = near(step)
+            base = pl.multiple_of(target * size, size)
+            back_out[tile, target] = products[pl.ds(base, size), :].astype(jnp.bfloat16)
+
+            @pl.when(step > 0)
+            def _():
+                back_copy(tile, target, seat).start()
+
+        each(0, team, give)
+        back_own(tile).start()
+
+    def finish(update, at, tile, tris):
+        tri = jnp.concatenate(tris, axis=1)
+        here = pl.ds(at, batch)
+        change = lax.dot_general(
+            normalise(tri, 0),
+            outw_v[update],
+            (((0,), (0,)), ((), ())),
+            preferred_element_type=jnp.float32,
+        )
+        flat = normed[here, tile].reshape(batch * lanes, channels)
+        gating = sigmoid(jnp.dot(flat, gate_v[update], preferred_element_type=jnp.float32))
+        values = cells[here, tile].reshape(batch * lanes, channels).astype(jnp.float32)
+        result = (values + gating * change).astype(jnp.bfloat16)
+        cells[here, tile] = result.reshape(batch, chips, pair_rows, channels)
+        return result
+
+    def team_arrived(copy, index):
+        each(1, team, lambda step: copy(index, seat, (seat + team - step) % team).wait_recv())
+
+    def consume_first(tile):
+        team_arrived(back_copy, tile)
+        back_own(tile).wait()
+        mask_tile = mask_v[:, tile * lanes : (tile + 1) * lanes]
+
+        def some_rows(step):
+            at = step * batch
+            tris = []
+            for which in range(batch):
+                base = pl.multiple_of((at + which) * per, per)
+                tri = back_in[tile, :, pl.ds(base, per), :].astype(jnp.float32)
+                tris.append(tri.reshape(team * per, lanes))
+            result = finish(0, at, tile, tris)
+            flat = normalise(result.astype(jnp.float32), 1)
+            normed[pl.ds(at, batch), tile] = flat.reshape(batch, lanes, channels)
+            gated = project(1, flat)
+            for which in range(batch):
+                mask = mask_s[mask_at(at + which)] * mask_tile
+                piece = (mask * gated[:, which * lanes : (which + 1) * lanes]).astype(jnp.bfloat16)
+                second_out[tile, :, at + which] = piece.reshape(team, 2 * per, lanes)
+
+        each(0, rows // batch, some_rows)
+        second_own(tile).start()
+        each(1, team, lambda step: second_copy(tile, near(step), seat).start())
+
+    def take_second(tile):
+        def put(source):
+            size = rows * 2 * per
+            block = second_in[tile, source].astype(jnp.float32).reshape(size, lanes)
+            wide[tile, pl.ds(pl.multiple_of(source * size, size), size), :] = block
+
+        def arrive(step):
+            source = (seat + team - step) % team
+            second_copy(tile, seat, source).wait_recv()
+            put(source)
+
+        second_own(tile).wait()
+        put(seat)
+        each(1, team, arrive)
+
+    block_rows = team * step_rows
+    block_size = block_rows * per
+    blocks = []
+    for newest in range(CHUNKS):
+        for older in range(newest):
+            blocks += [(older, newest), (newest, older)]
+        blocks.append((newest, newest))
+
+    def partial_block(block):
+        chunk, tile = blocks[block]
+        stride = 2 * per
+
+        def channel(index):
+            left = wide[chunk, pl.ds(index, team_rows, stride=stride), :]
+            right = wide[tile, pl.ds(per + index, team_rows, stride=stride), :]
+            tri = lax.dot_general(
+                left.astype(jnp.bfloat16),
+                right.astype(jnp.bfloat16),
+                (((0,), (0,)), ((), ())),
+                preferred_element_type=jnp.float32,
+            )
+            low, high = tri[:block_rows], tri[block_rows:]
+            lower = base_team == 0
+            products[pl.ds(block * block_size + index, block_rows, stride=per), :] = jnp.where(
+                lower, low, high
+            )
+            others[pl.ds(index, block_rows, stride=per), :] = jnp.where(lower, high, low)
+
+        each(0, per, channel)
+        cross_out[block] = others[...].astype(jnp.bfloat16)
+        cross_copy(block).start()
+
+    def combine(block):
+        cross_copy(block).wait_recv()
+        size = step_rows * per
+
+        def give(step):
+            target = near(step)
+            first = pl.multiple_of(target * size, size)
+            total = products[pl.ds(block * block_size + first, size), :] + cross_in[
+                block, pl.ds(first, size), :
+            ].astype(jnp.float32)
+            last_out[block, target] = total.astype(jnp.bfloat16)
+
+            @pl.when(step > 0)
+            def _():
+                last_copy(block, target, seat).start()
+
+        each(0, team, give)
+        last_own_copy(block).start()
+
+    def consume_second(block):
+        chunk, tile = blocks[block]
+        team_arrived(last_copy, block)
+        last_own_copy(block).wait()
+        for first in range(0, step_rows, batch):
+            tris = []
+            for which in range(first, first + batch):
+                tri = last_in[block, :, which * per : (which + 1) * per, :].astype(jnp.float32)
+                tris.append(tri.reshape(team * per, lanes))
+            finish(1, chunk * step_rows + first, tile, tris)
+        for copy in out_copies(chunk, tile):
+            copy.start()
+
+    grid = [(chunk, tile) for chunk in range(CHUNKS) for tile in range(tiles)]
+    for at in grid:
+        for copy in pair_copies(*at):
+            copy.start()
+    for chunk in range(CHUNKS):
+        for tile in range(tiles):
+            for copy in pair_copies(chunk, tile):
+                copy.wait()
+        produce_first(chunk)
+        if chunk == 0:
+            send_right(0)
+        send_left(chunk)
+    for chunk in range(1, CHUNKS):
+        send_right(chunk)
+    take_left()
+    for tile in range(tiles):
+        take_right(tile)
+        contract_first(tile)
+        if tile:
+            consume_first(tile - 1)
+    take_second(0)
+    partial_block(0)
+    consume_first(tiles - 1)
+    done = 1
+    for tile in range(1, tiles):
+        take_second(tile)
+        while done < (tile + 1) ** 2:
+            partial_block(done)
+            done += 1
+    for block in range(len(blocks)):
+        combine(block)
+        if block:
+            consume_second(block - 1)
+    consume_second(len(blocks) - 1)
+
+    for chunk in range(CHUNKS):
+
+        def sent(step):
+            left_copy(chunk, near(step), seat).wait_send()
+            right_copy(chunk, other_team + near(step), me).wait_send()
+            right_copy(chunk, base_team + near(step), me).wait_send()
+            back_copy(chunk, near(step), seat).wait_send()
+            second_copy(chunk, near(step), seat).wait_send()
+
+        right_copy(chunk, other_team + seat, me).wait_send()
+        each(1, team, sent)
+    for block in range(len(blocks)):
+        cross_copy(block).wait_send()
+        each(1, team, lambda step: last_copy(block, near(step), seat).wait_send())
+    for at in grid:
+        for copy in out_copies(*at):
+            copy.wait()
+
+
+def arrange(weight, groups):
+    channels, width = weight.shape
+    parts = weight.reshape(channels, 2, 2, groups, width // (4 * groups))
+    return parts.transpose(2, 3, 1, 4, 0).reshape(width, channels)
+
+
+def fused_shards(
+    pair, chain_ids, token_mask, same_chain_bias, proj_weight, gate_weight, out_weight
+):
+    rows_tile, cols_tile, channels = pair.shape
+    chips = lax.axis_size("row")
+    owners = 2 * chips
+    team = owners // 2
+    tokens = 2 * cols_tile
+    rows = rows_tile // 2
+    step_rows = rows // CHUNKS
+    hidden = proj_weight.shape[2] // 4
+    per = hidden // team
+    lanes = owners * step_rows
+    blocks = CHUNKS * CHUNKS
+    proj = jnp.stack([arrange(proj_weight[t], team) for t in range(2)])
+
+    def dealt(values):
+        parts = values.reshape(chips, CHUNKS, 2 * step_rows)
+        return parts.transpose(1, 0, 2).reshape(tokens)
+
+    chain_cols = jnp.broadcast_to(dealt(chain_ids)[:, None], (tokens, channels))
+    mask = token_mask.astype(jnp.float32)
+    bf16, f32 = jnp.bfloat16, jnp.float32
+    vmem = pl.BlockSpec(memory_space=pltpu.VMEM)
+    smem = pl.BlockSpec(memory_space=pltpu.SMEM)
+    anywhere = pl.BlockSpec(memory_space=pl.ANY)
+    view = (rows_tile, chips // 2, CHUNKS, 2 * step_rows, channels)
+
+    def sems(*shape):
+        return pltpu.SemaphoreType.DMA(shape)
+
+    result = pl.pallas_call(
+        functools.partial(fused_kernel, chips),
+        out_shape=jax.ShapeDtypeStruct(view, pair.dtype),
+        in_specs=[anywhere, smem, smem, vmem, vmem, vmem, vmem, vmem, vmem],
+        out_specs=anywhere,
+        scratch_shapes=[
+            pltpu.VMEM((rows, CHUNKS, chips, 2 * step_rows, channels), bf16),
+            pltpu.VMEM((rows, CHUNKS, lanes, channels), bf16),
+            pltpu.VMEM((team, rows, 2 * per, tokens), bf16),
+            pltpu.VMEM((team * rows, per, tokens), bf16),
+            pltpu.VMEM((CHUNKS, lanes, per, tokens), bf16),
+            pltpu.VMEM((CHUNKS, team * rows * 2 * per, lanes), f32),
+            pltpu.VMEM((blocks * team * step_rows * per, lanes), f32),
+            pltpu.VMEM((CHUNKS, team, rows * per, lanes), bf16),
+            pltpu.VMEM((CHUNKS, team, rows * per, lanes), bf16),
+            pltpu.VMEM((CHUNKS, team, rows, 2 * per, lanes), bf16),
+            pltpu.VMEM((CHUNKS, team, rows, 2 * per, lanes), bf16),
+            pltpu.VMEM((team * step_rows * per, lanes), f32),
+            pltpu.VMEM((blocks, team * step_rows * per, lanes), bf16),
+            pltpu.VMEM((blocks, team * step_rows * per, lanes), bf16),
+            pltpu.VMEM((blocks, team, step_rows * per, lanes), bf16),
+            pltpu.VMEM((blocks, team, step_rows * per, lanes), bf16),
+            sems(3, CHUNKS, CHUNKS),
+            sems(CHUNKS, team),
+            sems(CHUNKS, team),
+            sems(CHUNKS, owners),
+            sems(CHUNKS, owners),
+            sems(CHUNKS, team),
+            sems(CHUNKS, team),
+            sems(CHUNKS, team),
+            sems(CHUNKS, team),
+            sems(blocks),
+            sems(blocks),
+            sems(blocks, team),
+            sems(blocks, team),
+            sems(4, CHUNKS),
+            sems(blocks),
+            sems(3, CHUNKS, CHUNKS),
+        ],
+        compiler_params=pltpu.CompilerParams(
+            collective_id=0, has_side_effects=True, vmem_limit_bytes=60 * 1024 * 1024
+        ),
+    )(
+        pair.reshape(view),
+        chain_ids,
+        mask,
+        chain_cols,
+        dealt(mask)[None, :],
+        same_chain_bias.astype(f32)[None, :],
+        proj,
+        gate_weight,
+        out_weight,
+    )
+    return result.reshape(pair.shape)
+
+
+def fits(pair, proj_weight):
+    rows_tile, cols_tile, channels = pair.shape
+    rows_grid, cols_grid = lax.axis_size("row"), lax.axis_size("col")
+    hidden = proj_weight.shape[2] // 4
+    return (
+        cols_grid == 2
+        and rows_grid % 2 == 0
+        and hidden == 8 * cols_grid * rows_grid
+        and channels == 128
+        and rows_tile % (4 * CHUNKS) == 0
+        and cols_tile % 64 == 0
+        and rows_tile * rows_grid == 128 * CHUNKS
+        and rows_tile * rows_grid == cols_tile * cols_grid
+    )
+
+
+def program_shards(pair, chain_ids, token_mask, same_chain_bias, proj_weight, *rest):
+    chosen = fused_shards if fits(pair, proj_weight) else shards
+    return chosen(pair, chain_ids, token_mask, same_chain_bias, proj_weight, *rest)
+
+
 def solution(mesh):
     return jax.shard_map(
-        shards,
+        program_shards,
         mesh=mesh,
         in_specs=(P(("group", "row"), "col", None), P("group"), P("group"), P(), P(), P(), P()),
         out_specs=P(("group", "row"), "col", None),

time: 540 us -> 310 us (0.57); the launches traced: 533 us -> 308 us
  Pallas kernels: 0 us -> 299 us
  blocking collectives: 219 us -> 0 us
  local copies, waits for them, and re-layouts: 128 us -> 6.88 us
  waiting for transfers between devices: 94.2 us -> 0 us
  matrix products: 39.5 us -> 0 us
  other arithmetic: 40.3 us -> 2.59 us
  starting transfers between devices: 10.9 us -> 0 us
    pallas_call x0 -> x1, Pallas kernels: none -> 299 us  [fused_shards(): pl.pallas_call(functools.partial(fused_kernel, chips), out_shape=jax.Shap...]
    all_to_all x2 -> x0, blocking collectives: 219 us -> none  [triangle(): lax.all_to_all(stacked, ('row', 'col'), split_axis=0, concat_axis=0, tile...]
    all_to_all x2 -> x0, waiting for transfers between devices: 94.2 us -> none  [triangle(): lax.all_to_all(result, ('row', 'col'), split_axis=0, concat_axis=0, tiled...]
    reshape x10 -> x2, local copies, waits for them, and re-layouts: 76.4 us -> 0.85 us  [dealt(): parts = values.reshape(chips, CHUNKS, 2 * step_rows)]
    dot_general x8 -> x0, matrix products: 39.5 us -> none  [the longest x2 11.8 us: triangle(): jnp.dot(normed, gate, preferred_element_type=jnp.float32)]
    squeeze x4 -> x0, local copies, waits for them, and re-layouts: 20.6 us -> none  [the longest x2 14.8 us: contract(): whole[0]]
    convert_element_type x7 -> x1, other arithmetic: 19.1 us -> 0.68 us  [fused_shards(): mask = token_mask.astype(jnp.float32)]
    reduce_sum x7 -> x0, other arithmetic: 15.5 us -> none  [the longest x4 10.3 us: layer_norm(): var = jnp.mean(centred * centred, axis=-1, keepdims=True)]
  transfers between devices with their start and end apart: 2 -> 0, of which waited for: 2 -> 0; matrix products, arithmetic and copies ran while one was open for 2% -> 0% of each run, Pallas kernels for 0% -> 0%
where the time goes in v3:
time: 310 us; the launch traced here: 308 us
  Pallas kernels  299 us (96%)
  local copies, waits for them, and re-layouts  6.88 us (2%)
    pallas_call x1, Pallas kernels, fused_shards(): pl.pallas_call(functools.partial(fused_kernel, chips), out_shape=jax.Shap...  299 us

profile of v3, /device:TPU:15, one launch (start us, length us, event | category | flops | bytes accessed | tf_op | source)
XLA Modules:
  0.0 308.1 jit_solution(7063870480231584197)
XLA Ops:
  0.0 1.2 bitcast_convert_fusion.bias_v
  1.2 0.7 convert_element_type.4.mask_s
  1.9 0.0 copy-start
  1.9 0.1 reshape.15
  2.0 0.7 broadcast_in_dim_reshape.4.mask_v
  2.6 0.8 reshape.14
  3.4 0.1 broadcast_in_dim.12
  3.5 0.8 broadcast_in_dim.13.chain_v
  4.3 1.0 fusion
  5.3 0.1 copy.16
  5.4 0.1 copy.17
  5.6 0.7 pad_maximum_fusion.proj_v
  6.3 0.0 copy-done
  6.3 298.6 %shard_map.73 = bf16[48,4,3,16,128]{4,3,2,1,0:T(8,128)(2,1)} custom-call(bf16[48,4,3,16,128]{4,3,2,1,0:T(8,128)(2,1)} %bitcast.16, s32[384]{0:T(512)} %chain_s.1, f32[384]{0:T(512)} %copy-done, s32[384,128]{1,0:T(8,128)} %broadcast_in_dim.13.chain_v, f32[1,384]{1,0:T(1,128)} %broadcast_in_dim_reshape.4.mask_v, f32[1,128]{1,0:T(1,128)} %bitcast_convert_fusion.bias_v, ...), custom_call_target="tpu_custom_call" | custom-call | tf_op jit(solution)/shard_map/pallas_call | solution.py:623
  304.9 3.2 %copy.19 = bf16[48,192,128]{2,1,0:T(8,128)(2,1)} copy(bf16[48,192,128]{2,1,0:T(8,128)(2,1)} %bitcast.15) | data formatting | bytes 4718592
  (4 shorter events, 0.0 us)
Async XLA Ops:
  1.9 4.4 %copy-start = (f32[384]{0:T(512)}, f32[384]{0:T(512)S(1)}, u32[]{:S(2)}) copy-start(f32[384]{0:T(512)S(1)} %convert_element_type.4.mask_s) | copy-start | bytes 4612

commit v4 on v3

--- a/solution.py
+++ b/solution.py
@@ -101,6 +101,20 @@
     return (centred * lax.rsqrt(var + 1e-05)).astype(jnp.bfloat16)
 
 
+def block_order():
+    blocks, groups = [], []
+    for newest in range(CHUNKS):
+        first = len(blocks)
+        for older in range(newest):
+            blocks += [(older, newest), (newest, older)]
+        blocks.append((newest, newest))
+        cut = first + (len(blocks) - first) // 2 if newest == CHUNKS - 1 else len(blocks)
+        groups.append((first, cut, newest))
+        if cut < len(blocks):
+            groups.append((cut, len(blocks), newest))
+    return blocks, groups
+
+
 def fused_kernel(
     rows_grid,
     pair_ref,
@@ -124,9 +138,6 @@
     back_in,
     second_out,
     second_in,
-    others,
-    cross_out,
-    cross_in,
     last_out,
     last_in,
     pair_sems,
@@ -138,8 +149,6 @@
     back_recv,
     second_send,
     second_recv,
-    cross_send,
-    cross_recv,
     last_send,
     last_recv,
     own_sems,
@@ -162,6 +171,8 @@
     other_team = team - base_team
     sibling = {"row": row, "col": 1 - col}
     half_chips = chips // 2
+    share = team * per // owners
+    blocks, groups = block_order()
 
     def place(owner):
         return {"row": owner // 2, "col": owner % 2}
@@ -266,8 +277,27 @@
         )
 
     back_copy = functools.partial(team_copy, back_out, back_in, back_send, back_recv)
-    second_copy = functools.partial(team_copy, second_out, second_in, second_send, second_recv)
-    last_copy = functools.partial(team_copy, last_out, last_in, last_send, last_recv)
+
+    def second_copy(tile, target, source):
+        return pltpu.make_async_remote_copy(
+            src_ref=second_out.at[tile, target],
+            dst_ref=second_in.at[tile, source],
+            send_sem=second_send.at[tile, target],
+            recv_sem=second_recv.at[tile, source],
+            device_id=place(target),
+            device_id_type=MESH,
+        )
+
+    def last_copy(group, target, source):
+        span = pl.ds(groups[group][0], groups[group][1] - groups[group][0])
+        return pltpu.make_async_remote_copy(
+            src_ref=last_out.at[target, span],
+            dst_ref=last_in.at[source, span],
+            send_sem=last_send.at[group, target],
+            recv_sem=last_recv.at[group, source],
+            device_id=place(target),
+            device_id_type=MESH,
+        )
 
     def back_own(tile):
         return pltpu.make_async_copy(
@@ -276,23 +306,17 @@
 
     def second_own(tile):
         return pltpu.make_async_copy(
-            second_out.at[tile, seat], second_in.at[tile, seat], own_sems.at[3, tile]
-        )
-
-    def last_own_copy(block):
+            second_out.at[tile, me], second_in.at[tile, me], own_sems.at[3, tile]
+        )
+
+    def last_own_copy(group):
+        span = pl.ds(groups[group][0], groups[group][1] - groups[group][0])
         return pltpu.make_async_copy(
-            last_out.at[block, seat], last_in.at[block, seat], last_own.at[block]
-        )
-
-    def cross_copy(block):
-        return pltpu.make_async_remote_copy(
-            src_ref=cross_out.at[block],
-            dst_ref=cross_in.at[block],
-            send_sem=cross_send.at[block],
-            recv_sem=cross_recv.at[block],
-            device_id=place(other_team + seat),
-            device_id_type=MESH,
-        )
+            last_out.at[me, span], last_in.at[me, span], last_own.at[group]
+        )
+
+    def far(step):
+        return (me + step) % owners
 
     def near(step):
         return (seat + step) % team
@@ -422,11 +446,11 @@
         cells[here, tile] = result.reshape(batch, chips, pair_rows, channels)
         return result
 
-    def team_arrived(copy, index):
-        each(1, team, lambda step: copy(index, seat, (seat + team - step) % team).wait_recv())
+    def arrived(copy, index, people, own):
+        each(1, people, lambda step: copy(index, own, (own + people - step) % people).wait_recv())
 
     def consume_first(tile):
-        team_arrived(back_copy, tile)
+        arrived(back_copy, tile, team, seat)
         back_own(tile).wait()
         mask_tile = mask_v[:, tile * lanes : (tile + 1) * lanes]
 
@@ -444,90 +468,88 @@
             for which in range(batch):
                 mask = mask_s[mask_at(at + which)] * mask_tile
                 piece = (mask * gated[:, which * lanes : (which + 1) * lanes]).astype(jnp.bfloat16)
-                second_out[tile, :, at + which] = piece.reshape(team, 2 * per, lanes)
+                second_out[tile, :, at + which] = piece.reshape(owners, 2 * share, lanes)
 
         each(0, rows // batch, some_rows)
         second_own(tile).start()
-        each(1, team, lambda step: second_copy(tile, near(step), seat).start())
+        each(1, owners, lambda step: second_copy(tile, far(step), me).start())
 
     def take_second(tile):
         def put(source):
-            size = rows * 2 * per
+            size = rows * 2 * share
             block = second_in[tile, source].astype(jnp.float32).reshape(size, lanes)
             wide[tile, pl.ds(pl.multiple_of(source * size, size), size), :] = block
 
         def arrive(step):
-            source = (seat + team - step) % team
-            second_copy(tile, seat, source).wait_recv()
+            source = (me + owners - step) % owners
+            second_copy(tile, me, source).wait_recv()
             put(source)
 
         second_own(tile).wait()
-        put(seat)
-        each(1, team, arrive)
-
-    block_rows = team * step_rows
-    block_size = block_rows * per
-    blocks = []
-    for newest in range(CHUNKS):
-        for older in range(newest):
-            blocks += [(older, newest), (newest, older)]
-        blocks.append((newest, newest))
-
-    def partial_block(block):
-        chunk, tile = blocks[block]
-        stride = 2 * per
-
+        put(me)
+        each(1, owners, arrive)
+
+    block_size = lanes * share
+
+    def contract_second(newest):
         def channel(index):
-            left = wide[chunk, pl.ds(index, team_rows, stride=stride), :]
-            right = wide[tile, pl.ds(per + index, team_rows, stride=stride), :]
-            tri = lax.dot_general(
-                left.astype(jnp.bfloat16),
-                right.astype(jnp.bfloat16),
-                (((0,), (0,)), ((), ())),
-                preferred_element_type=jnp.float32,
-            )
-            low, high = tri[:block_rows], tri[block_rows:]
-            lower = base_team == 0
-            products[pl.ds(block * block_size + index, block_rows, stride=per), :] = jnp.where(
-                lower, low, high
-            )
-            others[pl.ds(index, block_rows, stride=per), :] = jnp.where(lower, high, low)
-
-        each(0, per, channel)
-        cross_out[block] = others[...].astype(jnp.bfloat16)
-        cross_copy(block).start()
-
-    def combine(block):
-        cross_copy(block).wait_recv()
-        size = step_rows * per
-
-        def give(step):
-            target = near(step)
-            first = pl.multiple_of(target * size, size)
-            total = products[pl.ds(block * block_size + first, size), :] + cross_in[
-                block, pl.ds(first, size), :
-            ].astype(jnp.float32)
-            last_out[block, target] = total.astype(jnp.bfloat16)
-
-            @pl.when(step > 0)
-            def _():
-                last_copy(block, target, seat).start()
-
-        each(0, team, give)
-        last_own_copy(block).start()
-
-    def consume_second(block):
-        chunk, tile = blocks[block]
-        team_arrived(last_copy, block)
-        last_own_copy(block).wait()
-        for first in range(0, step_rows, batch):
-            tris = []
-            for which in range(first, first + batch):
-                tri = last_in[block, :, which * per : (which + 1) * per, :].astype(jnp.float32)
-                tris.append(tri.reshape(team * per, lanes))
-            finish(1, chunk * step_rows + first, tile, tris)
-        for copy in out_copies(chunk, tile):
-            copy.start()
+            def side(tile, first):
+                values = wide[tile, pl.ds(first, tokens, stride=2 * share), :]
+                return values.astype(jnp.bfloat16)
+
+            def product(left, right):
+                return lax.dot_general(
+                    left, right, (((0,), (0,)), ((), ())), preferred_element_type=jnp.float32
+                )
+
+            def store(chunk, tile, tri):
+                first = blocks.index((chunk, tile)) * block_size
+                products[pl.ds(first + index, lanes, stride=share), :] = tri
+
+            lefts = [side(tile, index) for tile in range(newest + 1)]
+            rights = [side(tile, share + index) for tile in range(newest + 1)]
+            level = product(lefts[newest], jnp.concatenate(rights, axis=1))
+            for tile in range(newest + 1):
+                store(newest, tile, level[:, tile * lanes : (tile + 1) * lanes])
+            if newest:
+                upright = product(jnp.concatenate(lefts[:newest], axis=1), rights[newest])
+                for chunk in range(newest):
+                    store(chunk, newest, upright[chunk * lanes : (chunk + 1) * lanes])
+
+        each(0, share, channel)
+        size = step_rows * share
+        for group, (first, last, when) in enumerate(groups):
+            if when != newest:
+                continue
+
+            def give(step):
+                target = far(step)
+                for block in range(first, last):
+                    base = pl.multiple_of(block * block_size + target * size, size)
+                    last_out[target, block] = products[pl.ds(base, size), :].astype(jnp.bfloat16)
+
+                @pl.when(step > 0)
+                def _():
+                    last_copy(group, target, me).start()
+
+            each(0, owners, give)
+            last_own_copy(group).start()
+
+    def consume_second(group):
+        arrived(last_copy, group, owners, me)
+        last_own_copy(group).wait()
+        for block in range(groups[group][0], groups[group][1]):
+            chunk, tile = blocks[block]
+            for first in range(0, step_rows, batch):
+                tris = []
+                for which in range(first, first + batch, 2):
+                    two = last_in[:, block, which * share : (which + 2) * share, :]
+                    two = two.astype(jnp.float32)
+                    tris.append(two[:, :share].reshape(owners * share, lanes))
+                    tris.append(two[:, share:].reshape(owners * share, lanes))
+                finish(1, chunk * step_rows + first, tile, tris)
+            for copy in out_copies(chunk, tile):
+                copy.start()
 
     grid = [(chunk, tile) for chunk in range(CHUNKS) for tile in range(tiles)]
     for at in grid:
@@ -549,20 +571,12 @@
         contract_first(tile)
         if tile:
             consume_first(tile - 1)
-    take_second(0)
-    partial_block(0)
     consume_first(tiles - 1)
-    done = 1
-    for tile in range(1, tiles):
+    for tile in range(tiles):
         take_second(tile)
-        while done < (tile + 1) ** 2:
-            partial_block(done)
-            done += 1
-    for block in range(len(blocks)):
-        combine(block)
-        if block:
-            consume_second(block - 1)
-    consume_second(len(blocks) - 1)
+        contract_second(tile)
+    for group in range(len(groups)):
+        consume_second(group)
 
     for chunk in range(CHUNKS):
 
@@ -571,13 +585,13 @@
             right_copy(chunk, other_team + near(step), me).wait_send()
             right_copy(chunk, base_team + near(step), me).wait_send()
             back_copy(chunk, near(step), seat).wait_send()
-            second_copy(chunk, near(step), seat).wait_send()
 
         right_copy(chunk, other_team + seat, me).wait_send()
         each(1, team, sent)
-    for block in range(len(blocks)):
-        cross_copy(block).wait_send()
-        each(1, team, lambda step: last_copy(block, near(step), seat).wait_send())
+    for tile in range(tiles):
+        each(1, owners, lambda step: second_copy(tile, far(step), me).wait_send())
+    for group in range(len(groups)):
+        each(1, owners, lambda step: last_copy(group, far(step), me).wait_send())
     for at in grid:
         for copy in out_copies(*at):
             copy.wait()
@@ -602,8 +616,9 @@
     hidden = proj_weight.shape[2] // 4
     per = hidden // team
     lanes = owners * step_rows
-    blocks = CHUNKS * CHUNKS
-    proj = jnp.stack([arrange(proj_weight[t], team) for t in range(2)])
+    share = hidden // owners
+    blocks, groups = [len(part) for part in block_order()]
+    proj = jnp.stack([arrange(proj_weight[0], team), arrange(proj_weight[1], owners)])
 
     def dealt(values):
         parts = values.reshape(chips, CHUNKS, 2 * step_rows)
@@ -632,16 +647,13 @@
             pltpu.VMEM((team * rows, per, tokens), bf16),
             pltpu.VMEM((CHUNKS, lanes, per, tokens), bf16),
             pltpu.VMEM((CHUNKS, team * rows * 2 * per, lanes), f32),
-            pltpu.VMEM((blocks * team * step_rows * per, lanes), f32),
+            pltpu.VMEM((blocks * lanes * share, lanes), f32),
             pltpu.VMEM((CHUNKS, team, rows * per, lanes), bf16),
             pltpu.VMEM((CHUNKS, team, rows * per, lanes), bf16),
-            pltpu.VMEM((CHUNKS, team, rows, 2 * per, lanes), bf16),
-            pltpu.VMEM((CHUNKS, team, rows, 2 * per, lanes), bf16),
-            pltpu.VMEM((team * step_rows * per, lanes), f32),
-            pltpu.VMEM((blocks, team * step_rows * per, lanes), bf16),
-            pltpu.VMEM((blocks, team * step_rows * per, lanes), bf16),
-            pltpu.VMEM((blocks, team, step_rows * per, lanes), bf16),
-            pltpu.VMEM((blocks, team, step_rows * per, lanes), bf16),
+            pltpu.VMEM((CHUNKS, owners, rows, 2 * share, lanes), bf16),
+            pltpu.VMEM((CHUNKS, owners, rows, 2 * share, lanes), bf16),
+            pltpu.VMEM((owners, blocks, step_rows * share, lanes), bf16),
+            pltpu.VMEM((owners, blocks, step_rows * share, lanes), bf16),
             sems(3, CHUNKS, CHUNKS),
             sems(CHUNKS, team),
             sems(CHUNKS, team),
@@ -649,14 +661,12 @@
             sems(CHUNKS, owners),
             sems(CHUNKS, team),
             sems(CHUNKS, team),
-            sems(CHUNKS, team),
-            sems(CHUNKS, team),
-            sems(blocks),
-            sems(blocks),
-            sems(blocks, team),
-            sems(blocks, team),
+            sems(CHUNKS, owners),
+            sems(CHUNKS, owners),
+            sems(groups, owners),
+            sems(groups, owners),
             sems(4, CHUNKS),
-            sems(blocks),
+            sems(groups),
             sems(3, CHUNKS, CHUNKS),
         ],
         compiler_params=pltpu.CompilerParams(

time: 310 us -> 303 us (0.977)
  Pallas kernels: 299 us -> 294 us
    pallas_call x1, Pallas kernels: 299 us -> 294 us  [fused_shards(): pl.pallas_call(functools.partial(fused_kernel, chips), out_shape=jax.Shap...]
where the time goes in v4:
time: 303 us
  Pallas kernels  294 us (97%)
  local copies, waits for them, and re-layouts  6.9 us (2%)
    pallas_call x1, Pallas kernels, fused_shards(): pl.pallas_call(functools.partial(fused_kernel, chips), out_shape=jax.Shap...  294 us

profile of v4, /device:TPU:15, one launch (start us, length us, event | category | flops | bytes accessed | tf_op | source)
XLA Modules:
  0.0 303.1 jit_solution(7141924720179970246)
XLA Ops:
  0.0 1.2 bitcast_convert_fusion.bias_v
  1.2 0.7 convert_element_type.4.mask_s
  1.9 0.0 copy-start
  1.9 0.1 reshape.15
  2.0 0.7 broadcast_in_dim_reshape.4.mask_v
  2.6 0.8 reshape.14
  3.4 0.1 broadcast_in_dim.12
  3.5 0.8 broadcast_in_dim.13.chain_v
  4.3 1.0 fusion
  5.3 0.1 copy.16
  5.4 0.1 copy.17
  5.6 0.7 pad_maximum_fusion.proj_v
  6.3 0.0 copy-done
  6.3 293.6 %shard_map.73 = bf16[48,4,3,16,128]{4,3,2,1,0:T(8,128)(2,1)} custom-call(bf16[48,4,3,16,128]{4,3,2,1,0:T(8,128)(2,1)} %bitcast.16, s32[384]{0:T(512)} %chain_s.1, f32[384]{0:T(512)} %copy-done, s32[384,128]{1,0:T(8,128)} %broadcast_in_dim.13.chain_v, f32[1,384]{1,0:T(1,128)} %broadcast_in_dim_reshape.4.mask_v, f32[1,128]{1,0:T(1,128)} %bitcast_convert_fusion.bias_v, ...), custom_call_target="tpu_custom_call" | custom-call | tf_op jit(solution)/shard_map/pallas_call | solution.py:638
  299.9 3.2 %copy.19 = bf16[48,192,128]{2,1,0:T(8,128)(2,1)} copy(bf16[48,192,128]{2,1,0:T(8,128)(2,1)} %bitcast.15) | data formatting | bytes 4718592
  (4 shorter events, 0.0 us)
Async XLA Ops:
  1.9 4.5 %copy-start = (f32[384]{0:T(512)}, f32[384]{0:T(512)S(1)}, u32[]{:S(2)}) copy-start(f32[384]{0:T(512)S(1)} %convert_element_type.4.mask_s) | copy-start | bytes 4612

commit v5 on v4

--- a/solution.py
+++ b/solution.py
@@ -127,6 +127,7 @@
     gate_v,
     outw_v,
     out_ref,
+    turned,
     cells,
     normed,
     first_out,
@@ -336,27 +337,33 @@
 
     def project(update, flat):
         proj = lax.dot_general(
-            proj_v[update], flat, (((1,), (1,)), ((), ())), preferred_element_type=jnp.float32
-        )
-        width = proj.shape[0] // 2
-        return sigmoid(proj[width:]) * proj[:width]
+            turned[update], flat, (((1,), (1,)), ((), ())), preferred_element_type=jnp.float32
+        )
+        width = proj.shape[0] // 4
+        left = sigmoid(proj[width : 2 * width]) * proj[:width]
+        right = sigmoid(proj[3 * width :]) * proj[2 * width : 3 * width]
+        return left, right
 
     def mask_at(at):
         chunk, step = at // step_rows, at % step_rows
         return row * (2 * rows) + chunk * (2 * step_rows) + col * step_rows + step
 
     def produce_first(chunk):
+        bias = bias_v[...].astype(jnp.float32)
+
         def one_row(step):
             at = chunk * step_rows + step
             token = mask_at(at)
             values = cells[at].reshape(tokens, channels).astype(jnp.float32)
             same = chain_v[...] == chain_s[token]
-            start = (values + jnp.where(same, bias_v[...], 0.0)).astype(jnp.bfloat16)
+            start = (values + jnp.where(same, bias, 0.0)).astype(jnp.bfloat16)
             cells[at] = start.reshape(tiles, chips, pair_rows, channels)
             flat = normalise(start.astype(jnp.float32), 1)
             normed[at] = flat.reshape(tiles, lanes, channels)
-            gated = (mask_s[token] * mask_v[...]) * project(0, flat)
-            first_out[:, at] = gated.astype(jnp.bfloat16).reshape(team, 2 * per, tokens)
+            mask = mask_s[token].astype(jnp.float32) * mask_v[...]
+            for side, gated in enumerate(project(0, flat)):
+                piece = (mask * gated).astype(jnp.bfloat16).reshape(team, per, tokens)
+                first_out[:, at, side * per : (side + 1) * per] = piece
 
         each(0, step_rows, one_row)
 
@@ -464,11 +471,16 @@
             result = finish(0, at, tile, tris)
             flat = normalise(result.astype(jnp.float32), 1)
             normed[pl.ds(at, batch), tile] = flat.reshape(batch, lanes, channels)
-            gated = project(1, flat)
+            left, right = project(1, flat)
             for which in range(batch):
-                mask = mask_s[mask_at(at + which)] * mask_tile
-                piece = (mask * gated[:, which * lanes : (which + 1) * lanes]).astype(jnp.bfloat16)
-                second_out[tile, :, at + which] = piece.reshape(owners, 2 * share, lanes)
+                mask = mask_s[mask_at(at + which)].astype(jnp.float32) * mask_tile
+                span = slice(which * lanes, (which + 1) * lanes)
+                pieces = [
+                    (mask * gated[:, span]).reshape(owners, share, lanes)
+                    for gated in (left, right)
+                ]
+                piece = jnp.concatenate(pieces, axis=1).astype(jnp.bfloat16)
+                second_out[tile, :, at + which] = piece
 
         each(0, rows // batch, some_rows)
         second_own(tile).start()
@@ -555,6 +567,8 @@
     for at in grid:
         for copy in pair_copies(*at):
             copy.start()
+    for update in range(2):
+        turned[update] = proj_v[update].astype(jnp.float32).T.astype(jnp.bfloat16)
     for chunk in range(CHUNKS):
         for tile in range(tiles):
             for copy in pair_copies(chunk, tile):
@@ -597,12 +611,6 @@
             copy.wait()
 
 
-def arrange(weight, groups):
-    channels, width = weight.shape
-    parts = weight.reshape(channels, 2, 2, groups, width // (4 * groups))
-    return parts.transpose(2, 3, 1, 4, 0).reshape(width, channels)
-
-
 def fused_shards(
     pair, chain_ids, token_mask, same_chain_bias, proj_weight, gate_weight, out_weight
 ):
@@ -618,14 +626,12 @@
     lanes = owners * step_rows
     share = hidden // owners
     blocks, groups = [len(part) for part in block_order()]
-    proj = jnp.stack([arrange(proj_weight[0], team), arrange(proj_weight[1], owners)])
 
     def dealt(values):
         parts = values.reshape(chips, CHUNKS, 2 * step_rows)
         return parts.transpose(1, 0, 2).reshape(tokens)
 
     chain_cols = jnp.broadcast_to(dealt(chain_ids)[:, None], (tokens, channels))
-    mask = token_mask.astype(jnp.float32)
     bf16, f32 = jnp.bfloat16, jnp.float32
     vmem = pl.BlockSpec(memory_space=pltpu.VMEM)
     smem = pl.BlockSpec(memory_space=pltpu.SMEM)
@@ -641,6 +647,7 @@
         in_specs=[anywhere, smem, smem, vmem, vmem, vmem, vmem, vmem, vmem],
         out_specs=anywhere,
         scratch_shapes=[
+            pltpu.VMEM((2, 4 * hidden, channels), bf16),
             pltpu.VMEM((rows, CHUNKS, chips, 2 * step_rows, channels), bf16),
             pltpu.VMEM((rows, CHUNKS, lanes, channels), bf16),
             pltpu.VMEM((team, rows, 2 * per, tokens), bf16),
@@ -675,11 +682,11 @@
     )(
         pair.reshape(view),
         chain_ids,
-        mask,
+        token_mask,
         chain_cols,
-        dealt(mask)[None, :],
-        same_chain_bias.astype(f32)[None, :],
-        proj,
+        dealt(token_mask).astype(f32)[None, :],
+        same_chain_bias[None, :],
+        proj_weight,
         gate_weight,
         out_weight,
     )

time: 303 us -> 300 us (0.990)
  no operation moved by 1% of the time
where the time goes in v5:
time: 300 us
  Pallas kernels  293 us (98%)
  local copies, waits for them, and re-layouts  5.57 us (2%)
    pallas_call x1, Pallas kernels, fused_shards(): pl.pallas_call(functools.partial(fused_kernel, chips), out_shape=jax.Shap...  293 us

profile of v5, /device:TPU:15, one launch (start us, length us, event | category | flops | bytes accessed | tf_op | source)
XLA Modules:
  0.0 299.7 jit_solution(15220441993654342798)
XLA Ops:
  0.0 0.7 convert_element_type.19
  0.7 0.1 convert_element_type.20
  0.8 0.6 convert_element_type.22.mask_v
  1.4 0.8 reshape.25
  2.2 0.1 broadcast_in_dim.11
  2.2 0.8 broadcast_in_dim.12.chain_v
  3.0 293.5 %shard_map.73 = bf16[48,4,3,16,128]{4,3,2,1,0:T(8,128)(2,1)} custom-call(bf16[48,4,3,16,128]{4,3,2,1,0:T(8,128)(2,1)} %bitcast.6, s32[384]{0:T(512)} %chain_s.1, s32[384]{0:T(512)} %mask_s.1, s32[384,128]{1,0:T(8,128)} %broadcast_in_dim.12.chain_v, f32[1,384]{1,0:T(1,128)} %convert_element_type.22.mask_v, bf16[1,128]{1,0:T(2,128)(2,1)} %bitcast.9, ...), custom_call_target="tpu_custom_call" | custom-call | tf_op jit(solution)/shard_map/pallas_call | solution.py:644
  296.5 3.2 %copy.11 = bf16[48,192,128]{2,1,0:T(8,128)(2,1)} copy(bf16[48,192,128]{2,1,0:T(8,128)(2,1)} %bitcast.5) | data formatting | bytes 4718592
  (2 shorter events, 0.0 us)

commit v6 on v5

--- a/solution.py
+++ b/solution.py
@@ -108,10 +108,9 @@
         for older in range(newest):
             blocks += [(older, newest), (newest, older)]
         blocks.append((newest, newest))
-        cut = first + (len(blocks) - first) // 2 if newest == CHUNKS - 1 else len(blocks)
-        groups.append((first, cut, newest))
-        if cut < len(blocks):
-            groups.append((cut, len(blocks), newest))
+        run = 2 if newest == CHUNKS - 1 else len(blocks)
+        for start in range(first, len(blocks), run):
+            groups.append((start, min(start + run, len(blocks)), newest))
     return blocks, groups
 
 

time: 300 us -> 301 us (level)
  no operation moved by 1% of the time
where the time goes in v6:
time: 301 us; the launch traced here: 300 us
  Pallas kernels  293 us (97%)
  local copies, waits for them, and re-layouts  5.57 us (2%)
    pallas_call x1, Pallas kernels, fused_shards(): pl.pallas_call(functools.partial(fused_kernel, chips), out_shape=jax.Shap...  293 us

profile of v6, /device:TPU:15, one launch (start us, length us, event | category | flops | bytes accessed | tf_op | source)
XLA Modules:
  0.0 299.5 jit_solution(3082040414633494090)
XLA Ops:
  0.0 0.7 convert_element_type.19
  0.7 0.1 convert_element_type.20
  0.8 0.6 convert_element_type.22.mask_v
  1.4 0.8 reshape.25
  2.2 0.1 broadcast_in_dim.11
  2.2 0.8 broadcast_in_dim.12.chain_v
  3.0 293.2 %shard_map.73 = bf16[48,4,3,16,128]{4,3,2,1,0:T(8,128)(2,1)} custom-call(bf16[48,4,3,16,128]{4,3,2,1,0:T(8,128)(2,1)} %bitcast.6, s32[384]{0:T(512)} %chain_s.1, s32[384]{0:T(512)} %mask_s.1, s32[384,128]{1,0:T(8,128)} %broadcast_in_dim.12.chain_v, f32[1,384]{1,0:T(1,128)} %convert_element_type.22.mask_v, bf16[1,128]{1,0:T(2,128)(2,1)} %bitcast.9, ...), custom_call_target="tpu_custom_call" | custom-call | tf_op jit(solution)/shard_map/pallas_call | solution.py:643
  296.3 3.2 %copy.11 = bf16[48,192,128]{2,1,0:T(8,128)(2,1)} copy(bf16[48,192,128]{2,1,0:T(8,128)(2,1)} %bitcast.5) | data formatting | bytes 4718592
  (2 shorter events, 0.0 us)
